TPU v7x, 256 devices: a whole 4x4x8 slice. The times are simulated.
256 devices in a mesh: section: 4 (over y), group: 8 (over x, core), local: 8 (over z).
Axes of the slice: x: 4, y: 4, z: 8, core: 2. Of those that a mesh axis runs over, the one named last changes fastest.
Arguments:
- hidden_in: bfloat16 [4, 4096, 7168], P('section', ('group', 'local')), may hold values from -6 to 6
- norm_gain: bfloat16 [4, 7168], P('section'), may hold values from 0.099609375 to 1.8984375
- router: bfloat16 [4, 7168, 8], P('section'), may hold values from -0.0625 to 0.0625
- w_gate: bfloat16 [4, 8, 7168, 2048], P('section', 'group', None, 'local'), may hold values from -0.0625 to 0.0625
- w_up: bfloat16 [4, 8, 7168, 2048], P('section', 'group', None, 'local'), may hold values from -0.0625 to 0.0625
- w_down: bfloat16 [4, 8, 2048, 7168], P('section', 'group', 'local'), may hold values from -0.125 to 0.125
- routes: int32 [4, 4096, 2], P('section', ('group', 'local')), may hold values from 0 to 7, all different within a row; in each aligned block of 64 rows (0 to 63, 64 to 127, ..., all dimensions but the last counted through in order) at most 24 rows name the same one
Outputs:
- hidden_out: bfloat16 [4, 4096, 7168], P('section', ('group', 'local'))
Inputs may be any that keep to these rules, and one draw needn't show every extreme that they name: `routes`: each token names 2 different experts. Among the 64 tokens of one device (aligned blocks of tokens of one section), no expert is named more than 24 times, and in some blocks one expert is named exactly 24 times.
All inputs are finite; a program needn't handle non-finite values.
Results may differ from a plain program's by a relative error of at most 0.013.
Values may be sent and summed in bfloat16 or wider, within the bound.
A program may use at most 128 MiB of HBM per device.

v0:
```python
import jax
import jax.numpy as jnp
from jax import lax
from jax.sharding import PartitionSpec as P


def from_behind(shard, axis, by):
    count = lax.axis_size(axis)
    return lax.ppermute(shard, axis, [(i, (i + by) % count) for i in range(count)])


def norm_rows(incoming, gain_row):
    values = incoming.astype(jnp.float32)
    meansq = jnp.mean(values * values, axis=-1, keepdims=True)
    return (values * lax.rsqrt(meansq + 1e-06) * gain_row.astype(jnp.float32)).astype(jnp.bfloat16)


def route_gates(normed, router_matrix, choices_ids):
    logits = jnp.dot(normed, router_matrix, preferred_element_type=jnp.float32)
    affinity = jax.nn.sigmoid(logits)
    picked = jnp.take_along_axis(affinity, choices_ids, axis=1)
    return 2.5 * picked / jnp.sum(picked, axis=1, keepdims=True)


def slot_numbers(route_blocks, experts_total):
    onehot = (route_blocks[..., None] == jnp.arange(experts_total, dtype=jnp.int32)).astype(
        jnp.int32
    )
    earlier = jnp.cumsum(onehot, axis=-2) - onehot
    return jnp.sum(earlier * onehot, axis=-1)


def per_device(hidden_in, norm_gain, router, w_gate, w_up, w_down, routes):
    received = from_behind(hidden_in, "section", 1)
    incoming = received[0]
    tok_rows = incoming.shape[0]
    width = incoming.shape[1]
    choices_ids = routes[0]
    top_count = choices_ids.shape[1]
    experts_total = router.shape[2]
    group_count = lax.axis_size("group")
    local_count = lax.axis_size("local")
    capacity = min(tok_rows, 3 * tok_rows * top_count // (2 * experts_total))
    normed = norm_rows(incoming, norm_gain[0])
    gate_weights = route_gates(normed, router[0], choices_ids)
    local_slot = slot_numbers(choices_ids.reshape(1, -1), experts_total)[0]
    target = choices_ids.reshape(-1) * capacity + local_slot
    target_grid = target.reshape(tok_rows, top_count)
    slot_ids = jnp.arange(experts_total * capacity, dtype=jnp.int32)
    selector = jnp.any(slot_ids[:, None, None] == target_grid[None], axis=2).astype(jnp.bfloat16)
    dispatch = jnp.dot(selector, normed, preferred_element_type=jnp.float32).astype(jnp.bfloat16)
    dispatch = dispatch.reshape(experts_total, capacity, width)
    gate_matrix = w_gate[0, 0]
    up_matrix = w_up[0, 0]
    down_matrix = w_down[0, 0]
    copies = jnp.broadcast_to(dispatch[:, None], (experts_total, local_count, capacity, width))
    copies = copies.reshape(experts_total * local_count, capacity, width)
    arrived = lax.all_to_all(copies, ("group", "local"), split_axis=0, concat_axis=0, tiled=True)
    slot_rows = arrived.reshape(-1, width)
    gate_part = jnp.dot(slot_rows, gate_matrix, preferred_element_type=jnp.float32)
    up_part = jnp.dot(slot_rows, up_matrix, preferred_element_type=jnp.float32)
    active = (jax.nn.silu(gate_part) * up_part).astype(jnp.bfloat16)
    partial_value = (
        jnp.dot(active, down_matrix, preferred_element_type=jnp.float32)
        .astype(jnp.bfloat16)
        .reshape(-1, capacity, width)
    )
    came_back = lax.all_to_all(
        partial_value, ("group", "local"), split_axis=0, concat_axis=0, tiled=True
    )
    summed = jnp.sum(
        came_back.reshape(group_count, local_count, capacity, width).astype(jnp.float32), axis=1
    )
    returned = summed.astype(jnp.bfloat16)
    routed = (
        returned.reshape(-1, width)[target].reshape(tok_rows, top_count, width).astype(jnp.float32)
    )
    mixed_rows = incoming.astype(jnp.float32) + jnp.sum(gate_weights[..., None] * routed, axis=1)
    return mixed_rows.astype(jnp.bfloat16)[None]


def solution(mesh):
    placed = (
        P("section", ("group", "local"), None),
        P("section", None),
        P("section", None, None),
        P("section", "group", None, "local"),
        P("section", "group", None, "local"),
        P("section", "group", "local", None),
        P("section", ("group", "local"), None),
    )
    return jax.shard_map(
        per_device,
        mesh=mesh,
        in_specs=placed,
        out_specs=P("section", ("group", "local"), None),
        check_vma=False,
    )
```

profile of v0, /device:TPU:1, one launch (start us, length us, event | category | flops | bytes accessed | tf_op | source)
XLA Modules:
  0.0 1079.4 jit_solution(9909514339752098992)
XLA Ops:
  0.0 2.1 collective-permute-start
  2.1 0.8 mul.99
  2.9 0.8 copy.25
  3.9 0.2 reduce_window_sum.11
  4.1 0.2 select_reduce_fusion
  4.3 0.1 squeeze.25
  4.6 17.2 %collective-permute-done = bf16[1,64,7168]{2,1,0:T(8,128)(2,1)S(1)} collective-permute-done((bf16[1,64,7168]{2,1,0:T(8,128)(2,1)}, bf16[1,64,7168]{2,1,0:T(8,128)(2,1)S(1)}, u32[]{:S(2)}, u32[]{:S(2)}) %collective-permute-start) | collective-permute-done | bytes 917536 | tf_op jit(solution)/shard_map/ppermute | solution.py:9
  21.8 0.3 fusion.13
  22.1 1.0 convolution_convert_fusion.1
  23.1 2.3 broadcast_in_dim.10
  25.3 492.0 %all_to_all.10 = bf16[64,24,7168]{2,1,0:T(8,128)(2,1)S(1)} all-to-all(bf16[64,24,7168]{2,1,0:T(8,128)(2,1)S(1)} %bitcast.62), channel_id=1, replica_groups=mesh['section'=4,'group'=8,'local'=8] {'group','local'}, dimensions={0} | all-to-all | bytes 44040192 | tf_op jit(solution)/shard_map/all_to_all | solution.py:58
  517.3 9.5 fusion.3
  526.9 9.1 fusion.8
  536.0 12.7 %convolution_convert_fusion = bf16[1536,7168]{1,0:T(8,128)(2,1)} fusion(bf16[1536,256]{1,0:T(8,128)(2,1)S(1)} %fusion.8, bf16[1,1,256,7168]{3,2,1,0:T(8,128)(2,1)} %param.12), kind=kOutput, calls=%fused_computation.2 | convolution fusion | flops 5648154624 | bytes 26476544 | tf_op jit(solution)/shard_map/dot_general | solution.py:64
  548.7 7.2 all-to-all-start.1
  556.2 0.1 mul.97
  556.4 0.4 fusion.21
  556.8 1.0 gather_fusion.1
  558.2 492.4 %all-to-all-done.1 = bf16[64,24,7168]{2,1,0:T(8,128)(2,1)} async-done(((bf16[64,24,7168]{2,1,0:T(8,128)(2,1)}), bf16[64,24,7168]{2,1,0:T(8,128)(2,1)}, u32[]{:S(2)}, u32[]{:S(2)}) %all-to-all-start.1) | async-done | bytes 22020128 | tf_op jit(solution)/shard_map/all_to_all | solution.py:68
  1050.5 12.4 %bitcast_reduce_fusion = bf16[8,24,7168]{2,1,0:T(8,128)(2,1)S(1)} fusion(bf16[64,24,7168]{2,1,0:T(8,128)(2,1)} %all-to-all-done.1), kind=kLoop, calls=%fused_computation.3 | loop fusion | flops 9633792 | bytes 24772608 | tf_op jit(solution)/shard_map/reduce_sum | solution.py:71
  1063.0 3.0 gather_fusion
  1065.9 5.2 reshape.241
  1071.1 7.2 multiply_reduce_fusion
  1078.3 1.1 fusion.18
  (24 shorter events, 1.0 us)
Async XLA Ops:
  0.0 556.4 %copy-start = (bf16[1,7168,8]{1,2,0:T(8,128)(2,1)S(1)}, bf16[1,7168,8]{1,2,0:T(8,128)(2,1)}, u32[]{:S(2)}) copy-start(bf16[1,7168,8]{1,2,0:T(8,128)(2,1)} %param.9) | copy-start | bytes 344068
  0.0 21.8 %collective-permute-start = (bf16[1,64,7168]{2,1,0:T(8,128)(2,1)}, bf16[1,64,7168]{2,1,0:T(8,128)(2,1)S(1)}, u32[]{:S(2)}, u32[]{:S(2)}) collective-permute-start(bf16[1,64,7168]{2,1,0:T(8,128)(2,1)} %param.7), channel_id=1, source_target_pairs={{0,64},{64,128},{128,192},{192,0},{1,65},{65,129},{129,193},{193,1... | collective-permute-start | bytes 2752520 | tf_op jit(solution)/shard_map/ppermute | solution.py:9
  21.8 534.5 %copy-start.1 = (bf16[1,64,7168]{2,1,0:T(8,128)(2,1)}, bf16[1,64,7168]{2,1,0:T(8,128)(2,1)S(1)}, u32[]{:S(2)}) copy-start(bf16[1,64,7168]{2,1,0:T(8,128)(2,1)S(1)} %collective-permute-done) | copy-start | bytes 2752516
  548.7 7.2 copy-start.3
  548.7 501.9 %all-to-all-start.1 = ((bf16[64,24,7168]{2,1,0:T(8,128)(2,1)}), bf16[64,24,7168]{2,1,0:T(8,128)(2,1)}, u32[]{:S(2)}, u32[]{:S(2)}) async-start(bf16[64,24,7168]{2,1,0:T(8,128)(2,1)} %bitcast.61), calls=%async_computation.1 | async-start | bytes 44040192 | tf_op jit(solution)/shard_map/all_to_all | solution.py:68
  1071.1 7.2 copy-start.2
where the time goes:
time: 1100 us; the launch traced here: 1080 us
  waiting for transfers between devices  510 us (46%)
  blocking collectives  492 us (45%)
  matrix products  32.7 us (3%)
  other arithmetic  22.4 us (2%)
  local copies, waits for them, and re-layouts  13.3 us (1%)
    all_to_all x1, waiting for transfers between devices, per_device(): lax.all_to_all(partial_value, ('group', 'local'), split_axis=0, concat_ax...  492 us
    all_to_all x1, blocking collectives, per_device(): lax.all_to_all(copies, ('group', 'local'), split_axis=0, concat_axis=0, t...  492 us
  transfers between devices with their start and end apart: 2, of which 2 were waited for; matrix products, arithmetic and copies ran while one was open for 0% of the time, Pallas kernels for 0%

commit v1 on v0

v1 whole, which is shorter than its diff:
```python
import functools

import jax
import jax.numpy as jnp
from jax import lax
from jax.experimental import pallas as pl
from jax.experimental.pallas import tpu as pltpu
from jax.sharding import PartitionSpec as P

WIDTH = 7168
WIDTH_A = 3840
WIDTH_B = WIDTH - WIDTH_A
META = 128
WIDTH_BX = WIDTH_B + META
EXPERTS = 8
LOCALS = 8
ROWS = 64
CAP = 24
PAD = 32
SLOTS = EXPERTS * CAP
PAIRS = LOCALS // 2
HALF = 256
VMEM_BYTES = 63 * 2**20

BF16 = jnp.bfloat16
F32 = jnp.float32


def wrap(value, count=8):
    return lax.rem(value + 2 * count, count)


def spans(width, pieces):
    tiles = width // 128
    cuts = [128 * (tiles * i // pieces) for i in range(pieces + 1)]
    return [(cuts[i], cuts[i + 1] - cuts[i]) for i in range(pieces)]


def matmul(left, right):
    return jnp.dot(left, right, preferred_element_type=F32)


def enter(group, local):
    barrier = pltpu.get_barrier_semaphore()
    for step in (1, 7):
        pl.semaphore_signal(barrier, inc=1, device_id={"local": wrap(local + step)})
    for step in range(1, EXPERTS):
        pl.semaphore_signal(barrier, inc=1, device_id={"group": wrap(group + step)})
    pl.semaphore_wait(barrier, 2 + EXPERTS - 1)


def remote(src, dst, send, recv, device):
    return pltpu.make_async_remote_copy(
        src_ref=src, dst_ref=dst, send_sem=send, recv_sem=recv, device_id=device
    )


def hops_of(piece, pieces, way):
    first = piece < pieces // 2
    return 4 if first == (way == 0) else 3


def slot_masks(meta, columns, slot_of, expert_of, extra):
    out = []
    for choice in range(2):
        expert = meta[:, 2 * choice : 2 * choice + 1]
        slot = meta[:, 2 * choice + 1 : 2 * choice + 2]
        hit = (expert_of == expert) & (slot_of == slot)
        if extra is not None:
            hit = hit & extra
        out.append(hit)
    return out


def dispatch_kernel(
    disp_ref, tok_ref, wg_ref, wu_ref, acta_ref, actb_ref, meta_ref,
    xa, za, zb, xs, xr, hacc,
    xa_send, xa_recv, zb_send, zb_recv, za_send, za_recv, xb_send, xb_recv,
):
    group, local = lax.axis_index("group"), lax.axis_index("local")
    ring = ({"local": wrap(local + 1)}, {"local": wrap(local - 1)})
    sign = (1, -1)
    cuts_a, cuts_b = spans(WIDTH_A, 4), spans(WIDTH_BX, 2)
    enter(group, local)
    sent = []

    def start(copy):
        copy.start()
        sent.append(copy)

    def ring_copy(buffer, sends, recvs, cuts, way, hop, piece, src=None):
        begin, size = cuts[piece]
        block = wrap(local - sign[way] * (hop - 1))
        columns = pl.ds(begin, size)
        view = buffer.at[block, :, columns]
        return remote(
            view if src is None else src.at[:, columns],
            view,
            sends.at[way, hop - 1, piece],
            recvs.at[way, hop - 1, piece],
            ring[way],
        )

    def ring_step(buffer, sends, recvs, cuts, hop):
        for piece in range(len(cuts)):
            for way in range(2):
                hops = hops_of(piece, len(cuts), way)
                if hop <= hops:
                    ring_copy(buffer, sends, recvs, cuts, way, hop, piece).wait_recv()
                if hop < hops:
                    start(ring_copy(buffer, sends, recvs, cuts, way, hop + 1, piece))

    for piece in range(2):
        for way in range(2):
            start(ring_copy(zb, zb_send, zb_recv, cuts_b, way, 1, piece, tok_ref))
    xa_copies = []
    for step in range(1, EXPERTS):
        other = wrap(group + step)
        copy = remote(
            disp_ref.at[other], xa.at[group], xa_send.at[step], xa_recv.at[step], {"group": other}
        )
        start(copy)
        xa_copies.append(copy)
    zb[local] = tok_ref[...]
    xa[group] = disp_ref[group]

    ring_step(zb, zb_send, zb_recv, cuts_b, 1)
    ring_step(zb, zb_send, zb_recv, cuts_b, 2)
    ring_step(zb, zb_send, zb_recv, cuts_b, 3)
    for copy in xa_copies:
        copy.wait_recv()

    @pl.loop(0, WIDTH_A // HALF)
    def _(tile):
        columns = pl.ds(pl.multiple_of(tile * HALF, HALF), HALF)
        rows = xa[:, :, columns].astype(F32)
        za[local, :, columns] = rows[:, :CAP].reshape(SLOTS, HALF).astype(BF16)

    for piece in range(4):
        for way in range(2):
            start(ring_copy(za, za_send, za_recv, cuts_a, way, 1, piece))
    ring_step(zb, zb_send, zb_recv, cuts_b, 4)

    @pl.loop(0, PAIRS)
    def _(pair):
        meta = zb[pl.ds(2 * pair, 2), :, pl.ds(WIDTH_B, META)].reshape(2 * ROWS, META)
        meta_ref[pl.ds(2 * pair, 2)] = meta.reshape(2, ROWS, META)
        shape = (2 * ROWS, EXPERTS * 2 * CAP)
        column = lax.broadcasted_iota(jnp.int32, shape, 1)
        inside = lax.rem(column, 2 * CAP)
        owner = lax.broadcasted_iota(jnp.int32, shape, 0) // ROWS
        masks = slot_masks(
            meta.astype(F32),
            shape[1],
            lax.rem(inside, CAP).astype(F32),
            (column // (2 * CAP)).astype(F32),
            inside // CAP == owner,
        )
        selector = jnp.transpose((masks[0] | masks[1]).astype(F32)).astype(BF16)

        @pl.loop(0, WIDTH_B // HALF)
        def _(tile):
            columns = pl.ds(pl.multiple_of(tile * HALF, HALF), HALF)
            rows = zb[pl.ds(2 * pair, 2), :, columns].reshape(2 * ROWS, HALF)
            picked = matmul(selector, rows).astype(BF16).reshape(EXPERTS, 2 * CAP, HALF)
            xs[:, pl.ds(pl.multiple_of(pair * 2 * CAP, 2 * CAP), 2 * CAP), columns] = picked

    xb_copies = []
    for step in range(1, EXPERTS):
        other = wrap(group + step)
        copy = remote(xs.at[other], xr.at[group], xb_send.at[step], xb_recv.at[step], {"group": other})
        start(copy)
        xb_copies.append(copy)

    def add_a(block, _):
        block = wrap(block)
        rows = za[block]
        for half, weights in enumerate((wg_ref, wu_ref)):
            out = matmul(rows, weights[:WIDTH_A, :]).reshape(EXPERTS, CAP, HALF)
            hacc[block, :, :, half * HALF : (half + 1) * HALF] = out
        return _

    def add_b(source, owner):
        rows = source[owner]
        for half, weights in enumerate((wg_ref, wu_ref)):
            out = matmul(rows, weights[WIDTH_A:, :]).reshape(LOCALS, CAP, HALF)
            hacc[:, owner, :, half * HALF : (half + 1) * HALF] += out

    lax.fori_loop(local, local + 1, add_a, 0)
    for hop in range(1, 4):
        ring_step(za, za_send, za_recv, cuts_a, hop)
        lax.fori_loop(0, 2, lambda i, c, hop=hop: add_a(local - hop + 2 * hop * i, c), 0)
    ring_step(za, za_send, za_recv, cuts_a, 4)
    lax.fori_loop(local + 4, local + 5, add_a, 0)
    add_b(xs, group)
    for copy in xb_copies:
        copy.wait_recv()

    @pl.loop(1, EXPERTS)
    def _(step):
        add_b(xr, wrap(group - step))

    @pl.loop(0, LOCALS)
    def _(block):
        gate = hacc[block, :, :, :HALF]
        up = hacc[block, :, :, HALF:]
        active = jax.nn.silu(gate) * up
        hacc[block, :, :, :HALF] = active
        acta_ref[block] = active.reshape(SLOTS, HALF).astype(BF16)

    @pl.loop(0, EXPERTS)
    def _(owner):
        actb_ref[owner] = hacc[:, owner, :, :HALF].reshape(SLOTS, HALF).astype(BF16)

    for copy in sent:
        copy.wait_send()


def combine_kernel(
    acta_ref, actb_ref, wd_ref, meta_ref, inc_ref, out_ref,
    za, ru, rd, xs, xr, tb, tu, td, sb, ra,
    xb_send, xb_recv, za_send, za_recv, zb_send, zb_recv, xa_send, xa_recv,
):
    group, local = lax.axis_index("group"), lax.axis_index("local")
    ring = ({"local": wrap(local + 1)}, {"local": wrap(local - 1)})
    sign = (1, -1)
    cuts_a, cuts_b = spans(WIDTH_A, 4), spans(WIDTH_B, 2)
    enter(group, local)
    sent = []

    def start(copy):
        copy.start()
        sent.append(copy)

    def product_a(block):
        @pl.loop(0, WIDTH_A // HALF)
        def _(tile):
            columns = pl.ds(pl.multiple_of(tile * HALF, HALF), HALF)
            za[block, :, columns] = matmul(acta_ref[block], wd_ref[:, columns]).astype(BF16)

    def product_b(target, owner):
        @pl.loop(0, WIDTH_B // HALF)
        def _(tile):
            columns = pl.ds(pl.multiple_of(tile * HALF, HALF), HALF)
            weights = wd_ref[:, pl.ds(pl.multiple_of(WIDTH_A + tile * HALF, HALF), HALF)]
            target[owner, :, columns] = matmul(actb_ref[owner], weights).astype(BF16)

    def ring_copy(buffer, landed, sends, recvs, cuts, way, hop, piece):
        begin, size = cuts[piece]
        block = wrap(local + sign[way] * (5 - hop))
        columns = pl.ds(begin, size)
        return remote(
            buffer.at[block, :, columns],
            landed[way].at[hop - 1, :, columns],
            sends.at[way, hop - 1, piece],
            recvs.at[way, hop - 1, piece],
            ring[way],
        )

    def ring_step(buffer, landed, sends, recvs, cuts, hop):
        for piece in range(len(cuts)):
            for way in range(2):
                first = 5 - hops_of(piece, len(cuts), way)
                if hop < first:
                    continue
                if hop > first:
                    ring_copy(buffer, landed, sends, recvs, cuts, way, hop - 1, piece).wait_recv()
                    begin, size = cuts[piece]
                    columns = pl.ds(begin, size)
                    block = wrap(local + sign[way] * (5 - hop))
                    came = landed[way]
                    buffer[block, :, columns] += came[hop - 2, :, columns]
                start(ring_copy(buffer, landed, sends, recvs, cuts, way, hop, piece))

    ring_a = (za, (ru, rd), za_send, za_recv, cuts_a)
    ring_b = (tb, (tu, td), zb_send, zb_recv, cuts_b)

    product_a(wrap(local + 4))
    ring_step(*ring_a, 1)
    xb_copies = []
    for step in range(1, EXPERTS):
        other = wrap(group + step)
        product_b(xs, other)
        copy = remote(xs.at[other], xr.at[group], xb_send.at[step], xb_recv.at[step], {"group": other})
        start(copy)
        xb_copies.append(copy)
    for distance in (3, 2, 1):
        lax.fori_loop(
            0, 2, lambda i, c, d=distance: (product_a(wrap(local - d + 2 * d * i)), c)[1], 0
        )
        ring_step(*ring_a, 5 - distance)
    product_a(local)
    product_b(xr, group)
    sb[...] = jnp.zeros_like(sb)

    for copy in xb_copies:
        copy.wait_recv()

    @pl.loop(0, PAIRS)
    def _(pair):
        meta = meta_ref[pl.ds(2 * pair, 2)].reshape(2 * ROWS, META).astype(F32)
        shape = (2 * ROWS, EXPERTS * 2 * CAP)
        column = lax.broadcasted_iota(jnp.int32, shape, 1)
        inside = lax.rem(column, 2 * CAP)
        owner = lax.broadcasted_iota(jnp.int32, shape, 0) // ROWS
        masks = slot_masks(
            meta,
            shape[1],
            lax.rem(inside, CAP).astype(F32),
            (column // (2 * CAP)).astype(F32),
            inside // CAP == owner,
        )
        high, low = gate_matrices(meta, masks)

        @pl.loop(0, WIDTH_B // HALF)
        def _(tile):
            columns = pl.ds(pl.multiple_of(tile * HALF, HALF), HALF)
            rows = xr[:, pl.ds(pl.multiple_of(pair * 2 * CAP, 2 * CAP), 2 * CAP), columns]
            rows = rows.reshape(EXPERTS * 2 * CAP, HALF)
            mixed = matmul(high, rows) + matmul(low, rows)
            tb[pl.ds(2 * pair, 2), :, columns] = mixed.astype(BF16).reshape(2, ROWS, HALF)

    ring_step(*ring_b, 1)
    ring_step(*ring_b, 2)
    for piece in range(4):
        for way in range(2):
            ring_copy(*ring_a, way, 4, piece).wait_recv()

    @pl.loop(0, WIDTH_A // HALF)
    def _(tile):
        columns = pl.ds(pl.multiple_of(tile * HALF, HALF), HALF)
        total = (
            za[local, :, columns].astype(F32)
            + ru[3, :, columns].astype(F32)
            + rd[3, :, columns].astype(F32)
        ).reshape(EXPERTS, CAP, HALF)
        gap = jnp.zeros((EXPERTS, PAD - CAP, HALF), F32)
        sb[:, :, columns] = jnp.concatenate([total, gap], axis=1).astype(BF16)

    xa_copies = []
    for step in range(1, EXPERTS):
        other = wrap(group + step)
        copy = remote(sb.at[other], ra.at[group], xa_send.at[step], xa_recv.at[step], {"group": other})
        start(copy)
        xa_copies.append(copy)
    ra[group] = sb[group]
    ring_step(*ring_b, 3)
    ring_step(*ring_b, 4)

    meta = meta_ref[local].astype(F32)
    shape = (ROWS, EXPERTS * PAD)
    column = lax.broadcasted_iota(jnp.int32, shape, 1)
    masks = slot_masks(
        meta, shape[1], lax.rem(column, PAD).astype(F32), (column // PAD).astype(F32), None
    )
    high, low = gate_matrices(meta, masks)
    for copy in xa_copies:
        copy.wait_recv()

    @pl.loop(0, WIDTH_A // HALF)
    def _(tile):
        columns = pl.ds(pl.multiple_of(tile * HALF, HALF), HALF)
        rows = ra[:, :, columns].reshape(EXPERTS * PAD, HALF)
        mixed = matmul(high, rows) + matmul(low, rows)
        out_ref[:, columns] = (inc_ref[:, columns].astype(F32) + mixed).astype(BF16)

    for piece in range(2):
        for way in range(2):
            ring_copy(*ring_b, way, 4, piece).wait_recv()

    @pl.loop(0, WIDTH_B // HALF)
    def _(tile):
        columns = pl.ds(pl.multiple_of(tile * HALF, HALF), HALF)
        places = pl.ds(pl.multiple_of(WIDTH_A + tile * HALF, HALF), HALF)
        mixed = (
            tb[local, :, columns].astype(F32)
            + tu[3, :, columns].astype(F32)
            + td[3, :, columns].astype(F32)
        )
        out_ref[:, places] = (inc_ref[:, places].astype(F32) + mixed).astype(BF16)

    for copy in sent:
        copy.wait_send()


def gate_matrices(meta, masks):
    out = []
    for part in range(2):
        first, second = meta[:, 4 + part : 5 + part], meta[:, 6 + part : 7 + part]
        out.append((jnp.where(masks[0], first, 0.0) + jnp.where(masks[1], second, 0.0)).astype(BF16))
    return out


def norm_rows(incoming, gain_row):
    values = incoming.astype(F32)
    meansq = jnp.mean(values * values, axis=-1, keepdims=True)
    return (values * lax.rsqrt(meansq + 1e-06) * gain_row.astype(F32)).astype(BF16)


def route_gates(normed, router_matrix, choices_ids):
    logits = jnp.dot(normed, router_matrix, preferred_element_type=F32)
    affinity = jax.nn.sigmoid(logits)
    picked = jnp.take_along_axis(affinity, choices_ids, axis=1)
    return 2.5 * picked / jnp.sum(picked, axis=1, keepdims=True)


def slot_numbers(route_blocks, experts_total):
    onehot = (route_blocks[..., None] == jnp.arange(experts_total, dtype=jnp.int32)).astype(jnp.int32)
    earlier = jnp.cumsum(onehot, axis=-2) - onehot
    return jnp.sum(earlier * onehot, axis=-1)


def whole(shape, dtype=BF16):
    return pltpu.VMEM(shape, dtype)


def dma(*shape):
    return pltpu.SemaphoreType.DMA(shape)


def params(number):
    return pltpu.CompilerParams(
        collective_id=number, has_side_effects=True, vmem_limit_bytes=VMEM_BYTES
    )


def per_device(hidden_in, norm_gain, router, w_gate, w_up, w_down, routes):
    count = lax.axis_size("section")
    shifted = lax.ppermute(hidden_in, "section", [(i, (i + 1) % count) for i in range(count)])
    incoming = shifted[0]
    choices = routes[0]
    normed = norm_rows(incoming, norm_gain[0])
    gates = route_gates(normed, router[0], choices)
    slot = slot_numbers(choices.reshape(1, -1), EXPERTS)[0].reshape(ROWS, 2)

    place = choices * PAD + slot
    ids = jnp.arange(EXPERTS * PAD, dtype=jnp.int32)
    selector = jnp.any(ids[:, None, None] == place[None], axis=2).astype(BF16)
    disp = jnp.dot(selector, normed[:, :WIDTH_A], preferred_element_type=F32).astype(BF16)
    disp = disp.reshape(EXPERTS, PAD, WIDTH_A)

    high = gates.astype(BF16)
    low = (gates - high.astype(F32)).astype(BF16)
    meta = [choices[:, :1], slot[:, :1], choices[:, 1:], slot[:, 1:]]
    meta = [m.astype(BF16) for m in meta]
    meta += [high[:, :1], low[:, :1], high[:, 1:], low[:, 1:]]
    meta = jnp.concatenate(meta + [jnp.zeros((ROWS, META - 8), BF16)], axis=1)
    tokens = jnp.concatenate([normed[:, WIDTH_A:], meta], axis=1)

    vmem = pl.BlockSpec(memory_space=pltpu.VMEM)
    acta, actb, metas = pl.pallas_call(
        dispatch_kernel,
        out_shape=(
            jax.ShapeDtypeStruct((LOCALS, SLOTS, HALF), BF16),
            jax.ShapeDtypeStruct((EXPERTS, SLOTS, HALF), BF16),
            jax.ShapeDtypeStruct((LOCALS, ROWS, META), BF16),
        ),
        in_specs=[vmem] * 4,
        out_specs=(vmem,) * 3,
        scratch_shapes=[
            whole((EXPERTS, PAD, WIDTH_A)),
            whole((LOCALS, SLOTS, WIDTH_A)),
            whole((LOCALS, ROWS, WIDTH_BX)),
            whole((EXPERTS, SLOTS, WIDTH_B)),
            whole((EXPERTS, SLOTS, WIDTH_B)),
            whole((LOCALS, EXPERTS, CAP, 2 * HALF), F32),
            dma(8), dma(8), dma(2, 4, 2), dma(2, 4, 2), dma(2, 4, 4), dma(2, 4, 4), dma(8), dma(8),
        ],
        compiler_params=params(0),
        name="dispatch",
    )(disp, tokens, w_gate[0, 0], w_up[0, 0])

    mixed = pl.pallas_call(
        combine_kernel,
        out_shape=jax.ShapeDtypeStruct((ROWS, WIDTH), BF16),
        in_specs=[vmem] * 5,
        out_specs=vmem,
        scratch_shapes=[
            whole((LOCALS, SLOTS, WIDTH_A)),
            whole((4, SLOTS, WIDTH_A)),
            whole((4, SLOTS, WIDTH_A)),
            whole((EXPERTS, SLOTS, WIDTH_B)),
            whole((EXPERTS, SLOTS, WIDTH_B)),
            whole((LOCALS, ROWS, WIDTH_B)),
            whole((4, ROWS, WIDTH_B)),
            whole((4, ROWS, WIDTH_B)),
            whole((EXPERTS, PAD, WIDTH_A)),
            whole((EXPERTS, PAD, WIDTH_A)),
            dma(8), dma(8), dma(2, 4, 4), dma(2, 4, 4), dma(2, 4, 2), dma(2, 4, 2), dma(8), dma(8),
        ],
        compiler_params=params(1),
        name="combine",
    )(acta, actb, w_down[0, 0], metas, incoming)
    return mixed[None]


def solution(mesh):
    placed = (
        P("section", ("group", "local"), None),
        P("section", None),
        P("section", None, None),
        P("section", "group", None, "local"),
        P("section", "group", None, "local"),
        P("section", "group", "local", None),
        P("section", ("group", "local"), None),
    )
    return jax.shard_map(
        per_device,
        mesh=mesh,
        in_specs=placed,
        out_specs=P("section", ("group", "local"), None),
        check_vma=False,
    )
```

time: 1100 us -> 377 us (0.34); the launches traced: 1080 us -> 377 us
  waiting for transfers between devices: 510 us -> 14.6 us
  blocking collectives: 492 us -> 0 us
  Pallas kernels: 0 us -> 348 us
  matrix products: 32.7 us -> 2.42 us
  other arithmetic: 22.4 us -> 3.47 us
    all_to_all x1 -> x0, waiting for transfers between devices: 492 us -> none  [per_device(): lax.all_to_all(partial_value, ('group', 'local'), split_axis=0, concat_ax...]
    all_to_all x1 -> x0, blocking collectives: 492 us -> none  [per_device(): lax.all_to_all(copies, ('group', 'local'), split_axis=0, concat_axis=0, t...]
    pallas_call x0 -> x2, Pallas kernels: none -> 348 us  [the longest x1 181 us: per_device(): pl.pallas_call(dispatch_kernel, out_shape=(jax.ShapeDtypeStruct((LOCALS,...]
    dot_general x5 -> x2, matrix products: 32.7 us -> 2.42 us  [the longest x1 2 us: per_device(): jnp.dot(selector, normed[:, :WIDTH_A], preferred_element_type=F32)]
    reduce_sum x2 -> x0, other arithmetic: 19.6 us -> none  [the longest x1 12.4 us: per_device(): jnp.sum(came_back.reshape(group_count, local_count, capacity, width).asty...]
  transfers between devices with their start and end apart: 2 -> 1, of which waited for: 2 -> 1; matrix products, arithmetic and copies ran while one was open for 0% -> 1% of each run, Pallas kernels for 0% -> 0%
where the time goes in v1:
time: 377 us
  Pallas kernels  348 us (92%)
  waiting for transfers between devices  14.6 us (4%)
  local copies, waits for them, and re-layouts  6.67 us (2%)
    pallas_call x1, Pallas kernels, per_device(): pl.pallas_call(dispatch_kernel, out_shape=(jax.ShapeDtypeStruct((LOCALS,...  181 us
    pallas_call x1, Pallas kernels, per_device(): pl.pallas_call(combine_kernel, out_shape=jax.ShapeDtypeStruct((ROWS, WIDT...  167 us
    ppermute x1, waiting for transfers between devices, per_device(): lax.ppermute(hidden_in, 'section', [(i, (i + 1) % count) for i in range(c...  14.6 us
  transfers between devices with their start and end apart: 1, of which 1 were waited for; matrix products, arithmetic and copies ran while one was open for 1% of the time, Pallas kernels for 0%

profile of v1, /device:TPU:1, one launch (start us, length us, event | category | flops | bytes accessed | tf_op | source)
XLA Modules:
  0.0 377.0 jit_solution(9084612181342510168)
XLA Ops:
  0.0 2.1 collective-permute-start
  2.1 0.8 copy.37
  2.9 0.1 eq.43
  3.1 0.2 reduce_window_sum.11
  3.3 0.2 select_reduce_fusion
  3.5 0.1 reshape_squeeze.5
  3.6 0.8 mul.66
  4.4 0.7 fusion.17
  5.2 0.1 reshape.160
  5.3 0.8 copy.39
  6.1 0.1 reshape.159
  6.3 0.7 add_bitcast_fusion
  7.2 14.6 %collective-permute-done = bf16[1,64,7168]{2,1,0:T(8,128)(2,1)S(1)} collective-permute-done((bf16[1,64,7168]{2,1,0:T(8,128)(2,1)}, bf16[1,64,7168]{2,1,0:T(8,128)(2,1)S(1)}, u32[]{:S(2)}, u32[]{:S(2)}) %collective-permute-start) | collective-permute-done | bytes 917536 | tf_op jit(solution)/shard_map/ppermute | solution.py:429
  21.8 0.3 fusion
  22.1 0.4 fusion.5
  22.5 1.0 gather_fusion
  23.6 0.1 reshape.163
  23.7 0.1 fusion.18
  23.9 0.3 fusion.2
  24.3 2.0 convolution_convert_fusion
  26.3 0.9 concatenate.3.tok_ref
  27.2 180.6 %dispatch.1 = (bf16[8,192,256]{2,1,0:T(8,128)(2,1)}, bf16[8,192,256]{2,1,0:T(8,128)(2,1)}, bf16[8,64,128]{2,1,0:T(8,128)(2,1)}) custom-call(bf16[8,32,3840]{2,1,0:T(8,128)(2,1)} %bitcast.24, bf16[64,3456]{1,0:T(8,128)(2,1)} %concatenate.3.tok_ref, bf16[7168,256]{1,0:T(8,128)(2,1)} %bitcast.27, bf16[7168,256]{1,0:T(8,128)(2,1)} %bitcast.28), custom_call_target="tpu_custom_call" | custom-call | tf_op jit(solution)/shard_map/dispatch/pallas_call | solution.py:451
  207.8 167.0 %combine.1 = bf16[64,7168]{1,0:T(8,128)(2,1)} custom-call(bf16[8,192,256]{2,1,0:T(8,128)(2,1)} %get-tuple-element.8.acta_ref, bf16[8,192,256]{2,1,0:T(8,128)(2,1)} %get-tuple-element.9.actb_ref, bf16[256,7168]{1,0:T(8,128)(2,1)} %bitcast.26, bf16[8,64,128]{2,1,0:T(8,128)(2,1)} %get-tuple-element.10.meta_ref, bf16[64,7168]{1,0:T(8,128)(2,1)} %bitcast.23), custom_call_target="tpu_custom_call" | custom-call | tf_op jit(solution)/shard_map/combine/pallas_call | solution.py:473
  374.8 2.2 copy.45
  (16 shorter events, 0.7 us)
Async XLA Ops:
  0.0 22.1 %copy-start = (bf16[1,7168,8]{1,2,0:T(8,128)(2,1)S(1)}, bf16[1,7168,8]{1,2,0:T(8,128)(2,1)}, u32[]{:S(2)}) copy-start(bf16[1,7168,8]{1,2,0:T(8,128)(2,1)} %param.9) | copy-start | bytes 344068
  0.0 21.8 %collective-permute-start = (bf16[1,64,7168]{2,1,0:T(8,128)(2,1)}, bf16[1,64,7168]{2,1,0:T(8,128)(2,1)S(1)}, u32[]{:S(2)}, u32[]{:S(2)}) collective-permute-start(bf16[1,64,7168]{2,1,0:T(8,128)(2,1)} %param.7), channel_id=1, source_target_pairs={{0,64},{64,128},{128,192},{192,0},{1,65},{65,129},{129,193},{193,1... | collective-permute-start | bytes 2752520 | tf_op jit(solution)/shard_map/ppermute | solution.py:429
  21.8 2.1 copy-start.1

commit v2 on v0

v2 whole, which is shorter than its diff:
```python
import jax
import jax.numpy as jnp
from jax import lax
from jax.experimental import pallas as pl
from jax.experimental.pallas import tpu as pltpu
from jax.sharding import PartitionSpec as P

WIDTH = 7168
WIDTH_A = 3584
HALF_A = WIDTH_A // 2
WIDTH_B = WIDTH - WIDTH_A
META = 128
WIDTH_BX = WIDTH_B + META
EXPERTS = 8
LOCALS = 8
ROWS = 64
CAP = 24
TWICE = 2 * CAP
SLOTS = EXPERTS * CAP
PAIRS = LOCALS // 2
HIDDEN = 256
TILE = 256
CHUNKS = 4
CHUNK = ROWS // CHUNKS
PIECES = 4
VMEM_BYTES = 63 * 2**20

BF16 = jnp.bfloat16
F32 = jnp.float32


def wrap(value, count=8):
    return lax.rem(value + 2 * count, count)


def spans(width, pieces):
    tiles = width // 128
    cuts = [128 * (tiles * i // pieces) for i in range(pieces + 1)]
    return [(cuts[i], cuts[i + 1] - cuts[i]) for i in range(pieces)]


def matmul(left, right):
    return jnp.dot(left, right, preferred_element_type=F32)


def tile_at(tile, base=0):
    return pl.ds(pl.multiple_of(base + tile * TILE, TILE), TILE)


def pair_at(pair):
    return pl.ds(pl.multiple_of(pair * TWICE, TWICE), TWICE)


def remote(src, dst, send, recv, device):
    return pltpu.make_async_remote_copy(
        src_ref=src, dst_ref=dst, send_sem=send, recv_sem=recv, device_id=device
    )


def hops_of(piece, pieces, way):
    first = piece < pieces // 2
    return 4 if first == (way == 0) else 3


def pairs_near_first(local):
    own = local // 2
    odd = lax.rem(local, 2)
    return [own, wrap(own + 2 * odd - 1, PAIRS), wrap(own - 2 * odd + 1, PAIRS), wrap(own + 2, PAIRS)]


def slot_masks(meta, expert_of, slot_of):
    out = []
    for choice in range(2):
        expert = meta[:, 2 * choice : 2 * choice + 1]
        slot = meta[:, 2 * choice + 1 : 2 * choice + 2]
        out.append((expert_of == expert) & (slot_of == slot))
    return out


def pair_masks(meta):
    shape = (2 * ROWS, EXPERTS * TWICE)
    column = lax.broadcasted_iota(jnp.int32, shape, 1)
    inside = lax.rem(column, TWICE)
    owner = lax.broadcasted_iota(jnp.int32, shape, 0) // ROWS
    slot = jnp.where(inside // CAP == owner, lax.rem(inside, CAP), -1)
    return slot_masks(meta, (column // TWICE).astype(F32), slot.astype(F32))


def gate_matrices(meta):
    masks = pair_masks(meta)
    out = []
    for part in range(2):
        first, second = meta[:, 4 + part : 5 + part], meta[:, 6 + part : 7 + part]
        out.append((jnp.where(masks[0], first, 0.0) + jnp.where(masks[1], second, 0.0)).astype(BF16))
    return out


def dispatch_kernel(
    hid_ref, gain_ref, router_ref, routes_ref, wg_ref, wu_ref,
    acta_ref, actb_ref, meta_ref, inc_ref,
    inc, na, disp, xa, za, zb, xs, xr, hacc,
    y_send, y_recv, xa_send, xa_recv, zb_send, zb_recv, za_send, za_recv, xb_send, xb_recv,
):
    section = lax.axis_index("section")
    group, local = lax.axis_index("group"), lax.axis_index("local")
    ring = ({"local": wrap(local + 1)}, {"local": wrap(local - 1)})
    sign = (1, -1)
    cuts_a = spans(WIDTH_A, PIECES)
    pairs = pairs_near_first(local)
    sent = []

    barrier = pltpu.get_barrier_semaphore()
    pl.semaphore_signal(barrier, inc=1, device_id={"section": wrap(section - 1, 4)})
    for step in (1, 7):
        pl.semaphore_signal(barrier, inc=1, device_id={"local": wrap(local + step)})
    for step in range(1, EXPERTS):
        pl.semaphore_signal(barrier, inc=1, device_id={"group": wrap(group + step)})
    pl.semaphore_wait(barrier, 1 + 2 + EXPERTS - 1)

    def start(copy):
        copy.start()
        sent.append(copy)
        return copy

    def view_a(block, piece):
        begin, size = cuts_a[piece]
        return za.at[block, :, pl.ds(begin, size)]

    def view_b(block, piece):
        return zb.at[block, pl.ds(piece * CHUNK, CHUNK)]

    def ring_copy(kind, way, hop, piece):
        view, sends, recvs = kind
        there = view(wrap(local - sign[way] * (hop - 1)), piece)
        return remote(
            there, there, sends.at[way, hop - 1, piece], recvs.at[way, hop - 1, piece], ring[way]
        )

    def ring_step(kind, hop):
        for piece in range(4):
            for way in range(2):
                hops = hops_of(piece, 4, way)
                if hop <= hops:
                    ring_copy(kind, way, hop, piece).wait_recv()
                if hop < hops:
                    start(ring_copy(kind, way, hop + 1, piece))

    ring_a = (view_a, za_send, za_recv)
    ring_b = (view_b, zb_send, zb_recv)

    shifts = []
    for chunk in range(CHUNKS):
        rows = pl.ds(chunk * CHUNK, CHUNK)
        shifts.append(
            start(
                remote(
                    hid_ref.at[rows], inc.at[rows], y_send.at[chunk], y_recv.at[chunk],
                    {"section": wrap(section + 1, 4)},
                )
            )
        )

    lane = lax.broadcasted_iota(jnp.int32, (ROWS, META), 1)
    named = [routes_ref[:, choice : choice + 1] == lane for choice in range(2)]
    later = lax.broadcasted_iota(jnp.int32, (ROWS, ROWS), 0)
    earlier = lax.broadcasted_iota(jnp.int32, (ROWS, ROWS), 1)
    counts = (named[0].astype(F32) + named[1].astype(F32)).astype(BF16)
    before = matmul((later > earlier).astype(F32).astype(BF16), counts)
    meta = jnp.zeros((ROWS, META), F32)
    for choice in range(2):
        slot = jnp.sum(jnp.where(named[choice], before, 0.0), axis=1, keepdims=True)
        meta = jnp.where(lane == 2 * choice, routes_ref[:, choice : choice + 1].astype(F32), meta)
        meta = jnp.where(lane == 2 * choice + 1, slot, meta)

    for chunk in range(CHUNKS):
        shifts[chunk].wait_recv()
        rows = pl.ds(chunk * CHUNK, CHUNK)
        raw = inc[rows]
        inc_ref[rows] = raw
        values = raw.astype(F32)
        scale = lax.rsqrt(jnp.mean(values * values, axis=-1, keepdims=True) + 1e-06)
        normed = (values * scale * gain_ref[...].astype(F32)).astype(BF16)
        na[rows] = normed[:, :WIDTH_A]
        zb[local, rows, :WIDTH_B] = normed[:, WIDTH_A:]
        affinity = jax.nn.sigmoid(matmul(normed, router_ref[...]))
        part = meta[chunk * CHUNK : (chunk + 1) * CHUNK]
        expert = lax.broadcasted_iota(jnp.int32, (CHUNK, EXPERTS), 1).astype(F32)
        picked = [
            jnp.sum(
                jnp.where(part[:, 2 * choice : 2 * choice + 1] == expert, affinity, 0.0),
                axis=1,
                keepdims=True,
            )
            for choice in range(2)
        ]
        place = lane[:CHUNK]
        for choice in range(2):
            gate = 2.5 * picked[choice] / (picked[0] + picked[1])
            high = gate.astype(BF16).astype(F32)
            part = jnp.where(place == 4 + 2 * choice, high, part)
            part = jnp.where(place == 5 + 2 * choice, gate - high, part)
        zb[local, rows, WIDTH_B:] = part.astype(BF16)
        for way in range(2):
            start(ring_copy(ring_b, way, 1, chunk))

    column = lax.broadcasted_iota(jnp.int32, (ROWS, EXPERTS * 32), 1)
    masks = slot_masks(meta, (column // 32).astype(F32), lax.rem(column, 32).astype(F32))
    chosen = (masks[0] | masks[1]).astype(F32)
    chosen = jnp.transpose(jnp.concatenate([chosen, jnp.zeros_like(chosen)], axis=0))
    chosen = chosen.reshape(EXPERTS, 32, 2 * ROWS)[:, :CAP].reshape(SLOTS, 2 * ROWS)
    chosen = chosen[:, :ROWS].astype(BF16)

    @pl.loop(0, HALF_A // TILE)
    def _(tile):
        halves = [
            matmul(chosen, na[:, tile_at(tile, base)]).reshape(EXPERTS, CAP, TILE)
            for base in (0, HALF_A)
        ]
        disp[:, :, tile_at(tile)] = jnp.concatenate(halves, axis=1).astype(BF16)

    xa_copies = []
    for step in range(1, EXPERTS):
        other = wrap(group + step)
        copy = remote(
            disp.at[other], xa.at[group], xa_send.at[step], xa_recv.at[step], {"group": other}
        )
        xa_copies.append(start(copy))
    xa[group] = disp[group]

    def select(pair):
        meta = zb[pl.ds(2 * pair, 2), :, pl.ds(WIDTH_B, META)]
        meta_ref[pl.ds(2 * pair, 2)] = meta
        masks = pair_masks(meta.reshape(2 * ROWS, META).astype(F32))
        selector = jnp.transpose((masks[0] | masks[1]).astype(F32)).astype(BF16)

        @pl.loop(0, WIDTH_B // TILE)
        def _(tile):
            rows = zb[pl.ds(2 * pair, 2), :, tile_at(tile)].reshape(2 * ROWS, TILE)
            out = matmul(selector, rows).astype(BF16).reshape(EXPERTS, TWICE, TILE)
            xs[:, pair_at(pair), tile_at(tile)] = out

    xb_copies = []

    def send_pair(order):
        pair = pairs[order]
        select(pair)
        copies = []
        for step in range(1, EXPERTS):
            other = wrap(group + step)
            copy = remote(
                xs.at[other, pair_at(pair)], xr.at[group, pair_at(pair)],
                xb_send.at[order, step], xb_recv.at[order, step], {"group": other},
            )
            copies.append(start(copy))
        xb_copies.append(copies)
        xr[group, pair_at(pair)] = xs[group, pair_at(pair)]

    for hop in range(1, 4):
        ring_step(ring_b, hop)
        send_pair(hop - 1)
    for copy in xa_copies:
        copy.wait_recv()

    @pl.loop(0, HALF_A // TILE)
    def _(tile):
        rows = xa[:, :, tile_at(tile)].astype(F32)
        za[local, :, tile_at(tile)] = rows[:, :CAP].reshape(SLOTS, TILE).astype(BF16)
        za[local, :, tile_at(tile, HALF_A)] = rows[:, CAP:].reshape(SLOTS, TILE).astype(BF16)

    for piece in range(4):
        for way in range(2):
            start(ring_copy(ring_a, way, 1, piece))
    ring_step(ring_b, 4)
    send_pair(3)

    def add_a(block):
        block = wrap(block)
        rows = za[block]
        for half, weights in enumerate((wg_ref, wu_ref)):
            out = matmul(rows, weights[:WIDTH_A, :]).reshape(EXPERTS, CAP, HIDDEN)
            hacc[block, :, :, half * HIDDEN : (half + 1) * HIDDEN] = out

    def finish(pair):
        rows = xr[:, pair_at(pair), :].reshape(EXPERTS * TWICE, WIDTH_B)
        parts = []
        for half, weights in enumerate((wg_ref, wu_ref)):
            out = matmul(rows, weights[WIDTH_A:, :]).reshape(EXPERTS, 2, CAP, HIDDEN)
            done = [
                hacc[2 * pair + block, :, :, half * HIDDEN : (half + 1) * HIDDEN] + out[:, block]
                for block in range(2)
            ]
            parts.append(done)
        active = [jax.nn.silu(parts[0][block]) * parts[1][block] for block in range(2)]
        for block in range(2):
            acta_ref[2 * pair + block] = active[block].reshape(SLOTS, HIDDEN).astype(BF16)
        both = jnp.concatenate(active, axis=1)
        actb_ref[pair] = both.reshape(EXPERTS * TWICE, HIDDEN).astype(BF16)

    def blocks_of(hop):
        if hop == 0:
            return 1, lambda i: local
        if hop == 4:
            return 1, lambda i: local + 4
        return 2, lambda i: local - hop + 2 * hop * i

    def take(hop):
        count, place = blocks_of(hop)

        @pl.loop(0, count)
        def _(i):
            add_a(place(i))

    take(0)
    for hop in range(1, 5):
        ring_step(ring_a, hop)
        take(hop)
        for copy in xb_copies[hop - 1]:
            copy.wait_recv()
        finish(pairs[hop - 1])

    for copy in sent:
        copy.wait_send()


def combine_kernel(
    acta_ref, actb_ref, wd_ref, meta_ref, inc_ref, out_ref,
    za, ru, rd, hu, hd, xs, xr, tb, tu, td, sb, ra,
    xb_send, xb_recv, za_send, za_recv, zb_send, zb_recv, xa_send, xa_recv,
):
    group, local = lax.axis_index("group"), lax.axis_index("local")
    ring = ({"local": wrap(local + 1)}, {"local": wrap(local - 1)})
    sign = (1, -1)
    cuts_a, cuts_b = spans(WIDTH_A, PIECES), spans(WIDTH_B, 2)
    pairs = pairs_near_first(local)[::-1]
    sent = []

    barrier = pltpu.get_barrier_semaphore()
    for step in (1, 7):
        pl.semaphore_signal(barrier, inc=1, device_id={"local": wrap(local + step)})
    for step in range(1, EXPERTS):
        pl.semaphore_signal(barrier, inc=1, device_id={"group": wrap(group + step)})
    pl.semaphore_wait(barrier, 2 + EXPERTS - 1)

    def start(copy):
        copy.start()
        sent.append(copy)
        return copy

    def product_a(block):
        block = wrap(block)

        @pl.loop(0, WIDTH_A // TILE)
        def _(tile):
            za[block, :, tile_at(tile)] = matmul(acta_ref[block], wd_ref[:, tile_at(tile)]).astype(BF16)

    def product_both(distance):
        @pl.loop(0, 2)
        def _(i):
            product_a(local - distance + 2 * distance * i)

    def product_b(pair):
        @pl.loop(0, WIDTH_B // TILE)
        def _(tile):
            out = matmul(actb_ref[pair], wd_ref[:, tile_at(tile, WIDTH_A)]).astype(BF16)
            xs[:, pair_at(pair), tile_at(tile)] = out.reshape(EXPERTS, TWICE, TILE)

    def landing_a(way, hop, piece):
        begin, size = cuts_a[piece]
        if hop == 1:
            return (hu, hd)[way].at[:, pl.ds(begin - way * HALF_A, size)]
        return (ru, rd)[way].at[hop - 2, :, pl.ds(begin, size)]

    def landing_b(way, hop, piece):
        begin, size = cuts_b[piece]
        return (tu, td)[way].at[hop - 1, :, pl.ds(begin, size)]

    def ring_copy(kind, way, hop, piece):
        buffer, landing, sends, recvs, cuts = kind
        begin, size = cuts[piece]
        block = wrap(local + sign[way] * (5 - hop))
        return remote(
            buffer.at[block, :, pl.ds(begin, size)],
            landing(way, hop, piece),
            sends.at[way, hop - 1, piece],
            recvs.at[way, hop - 1, piece],
            ring[way],
        )

    def ring_open(kind, hop):
        for piece in range(len(kind[4])):
            for way in range(2):
                if hop == 5 - hops_of(piece, len(kind[4]), way):
                    start(ring_copy(kind, way, hop, piece))

    def ring_step(kind, hop):
        buffer, landing, _, _, cuts = kind
        for piece in range(len(cuts)):
            for way in range(2):
                if hop > 5 - hops_of(piece, len(cuts), way):
                    ring_copy(kind, way, hop - 1, piece).wait_recv()
                    begin, size = cuts[piece]
                    block = wrap(local + sign[way] * (5 - hop))
                    buffer[block, :, pl.ds(begin, size)] += landing(way, hop - 1, piece)[...]
                    start(ring_copy(kind, way, hop, piece))

    ring_a = (za, landing_a, za_send, za_recv, cuts_a)
    ring_b = (tb, landing_b, zb_send, zb_recv, cuts_b)
    xb_copies = []

    def send_pair(order):
        pair = pairs[order]
        product_b(pair)
        copies = []
        for step in range(1, EXPERTS):
            other = wrap(group + step)
            copy = remote(
                xs.at[other, pair_at(pair)], xr.at[group, pair_at(pair)],
                xb_send.at[order, step], xb_recv.at[order, step], {"group": other},
            )
            copies.append(start(copy))
        xb_copies.append(copies)
        xr[group, pair_at(pair)] = xs[group, pair_at(pair)]

    def mix_pair(order):
        pair = pairs[order]
        for copy in xb_copies[order]:
            copy.wait_recv()
        high, low = gate_matrices(meta_ref[pl.ds(2 * pair, 2)].reshape(2 * ROWS, META).astype(F32))

        @pl.loop(0, WIDTH_B // TILE)
        def _(tile):
            rows = xr[:, pair_at(pair), tile_at(tile)].reshape(EXPERTS * TWICE, TILE)
            mixed = matmul(high, rows) + matmul(low, rows)
            tb[pl.ds(2 * pair, 2), :, tile_at(tile)] = mixed.astype(BF16).reshape(2, ROWS, TILE)

    product_a(local + 4)
    ring_open(ring_a, 1)
    send_pair(0)
    product_both(3)
    ring_open(ring_a, 2)
    send_pair(1)
    ring_step(ring_a, 2)
    product_both(2)
    send_pair(2)
    ring_step(ring_a, 3)
    product_both(1)
    send_pair(3)
    product_a(local)
    mix_pair(0)
    ring_open(ring_b, 1)
    mix_pair(1)
    ring_open(ring_b, 2)
    ring_step(ring_b, 2)
    ring_step(ring_a, 4)
    mix_pair(2)
    for piece in range(PIECES):
        for way in range(2):
            ring_copy(ring_a, way, 4, piece).wait_recv()

    def total_a(columns):
        total = za[local, :, columns].astype(F32)
        total = total + ru[2, :, columns].astype(F32) + rd[2, :, columns].astype(F32)
        return total.reshape(EXPERTS, CAP, TILE)

    @pl.loop(0, HALF_A // TILE)
    def _(tile):
        halves = [total_a(tile_at(tile, base)) for base in (0, HALF_A)]
        sb[:, :, tile_at(tile)] = jnp.concatenate(halves, axis=1).astype(BF16)

    xa_copies = []
    for step in range(1, EXPERTS):
        other = wrap(group + step)
        copy = remote(
            sb.at[other], ra.at[group], xa_send.at[step], xa_recv.at[step], {"group": other}
        )
        xa_copies.append(start(copy))
    ra[group] = sb[group]
    ring_step(ring_b, 3)
    mix_pair(3)
    ring_step(ring_b, 4)

    own = meta_ref[local].astype(F32)
    high, low = gate_matrices(jnp.concatenate([own, own], axis=0))
    for copy in xa_copies:
        copy.wait_recv()

    @pl.loop(0, HALF_A // TILE)
    def _(tile):
        rows = ra[:, :, tile_at(tile)].reshape(EXPERTS * TWICE, TILE)
        mixed = matmul(high, rows) + matmul(low, rows)
        for half in range(2):
            columns = tile_at(tile, half * HALF_A)
            part = mixed[half * ROWS : (half + 1) * ROWS]
            out_ref[:, columns] = (inc_ref[:, columns].astype(F32) + part).astype(BF16)

    for piece in range(2):
        for way in range(2):
            ring_copy(ring_b, way, 4, piece).wait_recv()

    @pl.loop(0, WIDTH_B // TILE)
    def _(tile):
        columns, places = tile_at(tile), tile_at(tile, WIDTH_A)
        mixed = tb[local, :, columns].astype(F32)
        mixed = mixed + tu[3, :, columns].astype(F32) + td[3, :, columns].astype(F32)
        out_ref[:, places] = (inc_ref[:, places].astype(F32) + mixed).astype(BF16)

    for copy in sent:
        copy.wait_send()


def whole(*shape, dtype=BF16):
    return pltpu.VMEM(shape, dtype)


def dma(*shape):
    return pltpu.SemaphoreType.DMA(shape)


def params(number):
    return pltpu.CompilerParams(
        collective_id=number, has_side_effects=True, vmem_limit_bytes=VMEM_BYTES
    )


def per_device(hidden_in, norm_gain, router, w_gate, w_up, w_down, routes):
    vmem = pl.BlockSpec(memory_space=pltpu.VMEM)
    acta, actb, metas, incoming = pl.pallas_call(
        dispatch_kernel,
        out_shape=(
            jax.ShapeDtypeStruct((LOCALS, SLOTS, HIDDEN), BF16),
            jax.ShapeDtypeStruct((PAIRS, EXPERTS * TWICE, HIDDEN), BF16),
            jax.ShapeDtypeStruct((LOCALS, ROWS, META), BF16),
            jax.ShapeDtypeStruct((ROWS, WIDTH), BF16),
        ),
        in_specs=[vmem] * 6,
        out_specs=(vmem,) * 4,
        scratch_shapes=[
            whole(ROWS, WIDTH),
            whole(ROWS, WIDTH_A),
            whole(EXPERTS, TWICE, HALF_A),
            whole(EXPERTS, TWICE, HALF_A),
            whole(LOCALS, SLOTS, WIDTH_A),
            whole(LOCALS, ROWS, WIDTH_BX),
            whole(EXPERTS, SLOTS, WIDTH_B),
            whole(EXPERTS, SLOTS, WIDTH_B),
            whole(LOCALS, EXPERTS, CAP, 2 * HIDDEN, dtype=F32),
            dma(CHUNKS), dma(CHUNKS), dma(8), dma(8), dma(2, 4, 4), dma(2, 4, 4),
            dma(2, 4, 4), dma(2, 4, 4), dma(4, 8), dma(4, 8),
        ],
        compiler_params=params(0),
        name="dispatch",
    )(hidden_in[0], norm_gain, router[0], routes[0], w_gate[0, 0], w_up[0, 0])

    mixed = pl.pallas_call(
        combine_kernel,
        out_shape=jax.ShapeDtypeStruct((ROWS, WIDTH), BF16),
        in_specs=[vmem] * 5,
        out_specs=vmem,
        scratch_shapes=[
            whole(LOCALS, SLOTS, WIDTH_A),
            whole(3, SLOTS, WIDTH_A),
            whole(3, SLOTS, WIDTH_A),
            whole(SLOTS, HALF_A),
            whole(SLOTS, HALF_A),
            whole(EXPERTS, SLOTS, WIDTH_B),
            whole(EXPERTS, SLOTS, WIDTH_B),
            whole(LOCALS, ROWS, WIDTH_B),
            whole(4, ROWS, WIDTH_B),
            whole(4, ROWS, WIDTH_B),
            whole(EXPERTS, TWICE, HALF_A),
            whole(EXPERTS, TWICE, HALF_A),
            dma(4, 8), dma(4, 8), dma(2, 4, 4), dma(2, 4, 4), dma(2, 4, 2), dma(2, 4, 2),
            dma(8), dma(8),
        ],
        compiler_params=params(1),
        name="combine",
    )(acta, actb, w_down[0, 0], metas, incoming)
    return mixed[None]


def solution(mesh):
    placed = (
        P("section", ("group", "local"), None),
        P("section", None),
        P("section", None, None),
        P("section", "group", None, "local"),
        P("section", "group", None, "local"),
        P("section", "group", "local", None),
        P("section", ("group", "local"), None),
    )
    return jax.shard_map(
        per_device,
        mesh=mesh,
        in_specs=placed,
        out_specs=P("section", ("group", "local"), None),
        check_vma=False,
    )
```

time: 1100 us -> 335 us (0.30); the launches traced: 1080 us -> 335 us
  waiting for transfers between devices: 510 us -> 0 us
  blocking collectives: 492 us -> 0 us
  Pallas kernels: 0 us -> 329 us
  matrix products: 32.7 us -> 0 us
  other arithmetic: 22.4 us -> 0 us
    all_to_all x1 -> x0, waiting for transfers between devices: 492 us -> none  [per_device(): lax.all_to_all(partial_value, ('group', 'local'), split_axis=0, concat_ax...]
    all_to_all x1 -> x0, blocking collectives: 492 us -> none  [per_device(): lax.all_to_all(copies, ('group', 'local'), split_axis=0, concat_axis=0, t...]
    pallas_call x0 -> x2, Pallas kernels: none -> 329 us  [the longest x1 177 us: per_device(): pl.pallas_call(dispatch_kernel, out_shape=(jax.ShapeDtypeStruct((LOCALS,...]
    dot_general x5 -> x0, matrix products: 32.7 us -> none  [the longest x1 12.7 us: per_device(): jnp.dot(active, down_matrix, preferred_element_type=jnp.float32)]
    reduce_sum x5 -> x0, other arithmetic: 20.1 us -> none  [the longest x1 12.4 us: per_device(): jnp.sum(came_back.reshape(group_count, local_count, capacity, width).asty...]
    ppermute x1 -> x0, waiting for transfers between devices: 17.2 us -> none  [from_behind(): lax.ppermute(shard, axis, [(i, (i + by) % count) for i in range(count)])]
  transfers between devices with their start and end apart: 2 -> 0, of which waited for: 2 -> 0; matrix products, arithmetic and copies ran while one was open for 0% -> 0% of each run, Pallas kernels for 0% -> 0%
where the time goes in v2:
time: 335 us
  Pallas kernels  329 us (98%)
  local copies, waits for them, and re-layouts  5.96 us (2%)
    pallas_call x1, Pallas kernels, per_device(): pl.pallas_call(dispatch_kernel, out_shape=(jax.ShapeDtypeStruct((LOCALS,...  177 us
    pallas_call x1, Pallas kernels, per_device(): pl.pallas_call(combine_kernel, out_shape=jax.ShapeDtypeStruct((ROWS, WIDT...  153 us

profile of v2, /device:TPU:1, one launch (start us, length us, event | category | flops | bytes accessed | tf_op | source)
XLA Modules:
  0.0 335.2 jit_solution(14087168554365761985)
XLA Ops:
  0.0 1.4 copy.9.routes_ref
  1.4 2.4 copy.8
  3.8 176.6 %dispatch.1 = (bf16[8,192,256]{2,1,0:T(8,128)(2,1)}, bf16[4,384,256]{2,1,0:T(8,128)(2,1)}, bf16[8,64,128]{2,1,0:T(8,128)(2,1)}, bf16[64,7168]{1,0:T(8,128)(2,1)}) custom-call(bf16[64,7168]{1,0:T(8,128)(2,1)} %bitcast.12, bf16[1,7168]{1,0:T(2,128)(2,1)} %gain_ref.1, bf16[7168,8]{1,0:T(8,128)(2,1)} %bitcast.7, s32[64,2]{1,0:T(8,128)} %copy.9.routes_ref, ...), custom_call_target="tpu_custom_call" | custom-call | tf_op jit(solution)/shard_map/dispatch/pallas_call | solution.py:527
  180.4 152.6 %combine.1 = bf16[64,7168]{1,0:T(8,128)(2,1)} custom-call(bf16[8,192,256]{2,1,0:T(8,128)(2,1)} %get-tuple-element.9.acta_ref, bf16[4,384,256]{2,1,0:T(8,128)(2,1)} %get-tuple-element.10.actb_ref, bf16[256,7168]{1,0:T(8,128)(2,1)} %bitcast.9, bf16[8,64,128]{2,1,0:T(8,128)(2,1)} %get-tuple-element.11.meta_ref, bf16[64,7168]{1,0:T(8,128)(2,1)} %get-tuple-element.12.inc_ref), custom_call_target="tpu_custom_call" | custom-call | tf_op jit(solution)/shard_map/combine/pallas_call | solution.py:554
  333.0 2.2 copy.11

commit v3 on v0

v3 whole, which is shorter than its diff:
```python
import jax
import jax.numpy as jnp
from jax import lax
from jax.experimental import pallas as pl
from jax.experimental.pallas import tpu as pltpu
from jax.sharding import PartitionSpec as P

WIDTH = 7168
WIDTH_A = 3584
WIDTH_B = WIDTH - WIDTH_A
HALF = 1792
QUARTER = 896
META = 128
WIDTH_BX = META + WIDTH_B + META
GATES_AT = META + WIDTH_B
EXPERTS = 8
LOCALS = 8
SECTIONS = 4
ROWS = 64
CAP = 24
TWICE = 2 * CAP
SLOTS = EXPERTS * CAP
PAIRS = LOCALS // 2
HIDDEN = 256
TILE = 256
LANES = 128
VMEM_BYTES = 63 * 2**20

BF16 = jnp.bfloat16
F32 = jnp.float32


def wrap(value, count=8):
    return lax.rem(value + 2 * count, count)


def matmul(left, right):
    return jnp.dot(left, right, preferred_element_type=F32)


def lanes_at(start, size):
    return pl.ds(pl.multiple_of(start, LANES), size)


def pair_at(pair):
    return pl.ds(pl.multiple_of(pair * TWICE, TWICE), TWICE)


def remote(src, dst, send, recv, device):
    return pltpu.make_async_remote_copy(
        src_ref=src, dst_ref=dst, send_sem=send, recv_sem=recv, device_id=device
    )


def hops_of(piece, pieces, way):
    first = piece < pieces // 2
    return 4 if first == (way == 0) else 3


def pairs_near_first(local):
    own = local // 2
    odd = lax.rem(local, 2)
    return [own, wrap(own + 2 * odd - 1, PAIRS), wrap(own - 2 * odd + 1, PAIRS), wrap(own + 2, PAIRS)]


def slot_masks(meta, expert_of, slot_of):
    out = []
    for choice in range(2):
        expert = meta[:, 2 * choice : 2 * choice + 1]
        slot = meta[:, 2 * choice + 1 : 2 * choice + 2]
        out.append((expert_of == expert) & (slot_of == slot))
    return out


def pair_masks(meta):
    shape = (2 * ROWS, EXPERTS * TWICE)
    column = lax.broadcasted_iota(jnp.int32, shape, 1)
    inside = lax.rem(column, TWICE)
    owner = lax.broadcasted_iota(jnp.int32, shape, 0) // ROWS
    slot = jnp.where(inside // CAP == owner, lax.rem(inside, CAP), -1)
    return slot_masks(meta, (column // TWICE).astype(F32), slot.astype(F32))


def gate_matrices(meta, gates):
    masks = pair_masks(meta)
    out = []
    for part in range(2):
        first, second = gates[:, part : 1 + part], gates[:, 2 + part : 3 + part]
        out.append((jnp.where(masks[0], first, 0.0) + jnp.where(masks[1], second, 0.0)).astype(BF16))
    return out


def layer_kernel(
    hid_ref, gain_ref, router_ref, routes_ref, wg_hbm, wu_hbm, wd_hbm, out_ref,
    wg, wu, wd, inc, scale_out, scale_in, na, disp, xa, za, zd, zb, xs, xr, hacc, acta, actb, tu, td,
    w_sem, y_send, y_recv, xa_send, xa_recv, zb_send, zb_recv, za_send, za_recv, xb_send, xb_recv,
    free_x, free_z,
    xc_send, xc_recv, zc_send, zc_recv, ze_send, ze_recv, xe_send, xe_recv,
):
    section = lax.axis_index("section")
    group, local = lax.axis_index("group"), lax.axis_index("local")
    ring = ({"local": wrap(local + 1)}, {"local": wrap(local - 1)})
    after = {"section": wrap(section + 1, SECTIONS)}
    sign = (1, -1)
    pairs = pairs_near_first(local)

    barrier = pltpu.get_barrier_semaphore()
    pl.semaphore_signal(barrier, inc=1, device_id={"section": wrap(section - 1, SECTIONS)})
    for way in range(2):
        pl.semaphore_signal(barrier, inc=1, device_id=ring[way])
    for step in range(1, EXPERTS):
        pl.semaphore_signal(barrier, inc=1, device_id={"group": wrap(group + step)})
    loads = [
        pltpu.make_async_copy(hbm, here, w_sem.at[i])
        for i, (hbm, here) in enumerate(((wg_hbm, wg), (wu_hbm, wu), (wd_hbm, wd)))
    ]
    for load in loads:
        load.start()
    pl.semaphore_wait(barrier, 1 + 2 + EXPERTS - 1)

    def start(copy, into):
        copy.start()
        into.append(copy)
        return copy


    chunks = (WIDTH_A, 0, HALF, WIDTH_A + HALF)
    shifts = []
    for number, begin in enumerate(chunks):
        view = pl.ds(begin, HALF)
        shifts.append(
            remote(hid_ref.at[:, view], inc.at[:, view], y_send.at[number], y_recv.at[number], after)
        )
    shifts[0].start()
    squares = jnp.zeros((ROWS, 1), F32)
    for begin in chunks:
        values = hid_ref[:, pl.ds(begin, HALF)].astype(F32)
        squares = squares + jnp.sum(values * values, axis=-1, keepdims=True)
    scale_out[...] = jnp.broadcast_to(lax.rsqrt(squares / WIDTH + 1e-06), (ROWS, LANES))
    scale_copy = remote(scale_out, scale_in, y_send.at[4], y_recv.at[4], after)
    scale_copy.start()
    shifts[1].start()

    square = (ROWS, ROWS)
    down, across = lax.broadcasted_iota(jnp.int32, square, 0), lax.broadcasted_iota(jnp.int32, square, 1)
    lane = lax.broadcasted_iota(jnp.int32, (ROWS, META), 1)
    experts = []
    for choice in range(2):
        row = jnp.broadcast_to(routes_ref[choice : choice + 1, :].astype(F32), square)
        experts.append(jnp.sum(jnp.where(down == across, row, 0.0), axis=1, keepdims=True))
    named = [expert == lane.astype(F32) for expert in experts]
    counts = (named[0].astype(F32) + named[1].astype(F32)).astype(BF16)
    before = matmul((down > across).astype(F32).astype(BF16), counts)
    meta = jnp.zeros((ROWS, META), F32)
    for choice in range(2):
        slot = jnp.sum(jnp.where(named[choice], before, 0.0), axis=1, keepdims=True)
        meta = jnp.where(lane == 2 * choice, experts[choice], meta)
        meta = jnp.where(lane == 2 * choice + 1, slot, meta)

    column = lax.broadcasted_iota(jnp.int32, (ROWS, EXPERTS * 32), 1)
    masks = slot_masks(meta, (column // 32).astype(F32), lax.rem(column, 32).astype(F32))
    chosen = (masks[0] | masks[1]).astype(F32)
    chosen = jnp.transpose(jnp.concatenate([chosen, jnp.zeros_like(chosen)], axis=0))
    chosen = chosen.reshape(EXPERTS, 32, 2 * ROWS)[:, :CAP].reshape(SLOTS, 2 * ROWS)
    chosen = chosen[:, :ROWS].astype(BF16)

    def normed_chunk(number):
        shifts[number].wait_recv()
        if number + 2 < len(shifts):
            shifts[number].wait_send()
            shifts[number + 2].start()
        if number == 0:
            scale_copy.wait_recv()
        view = pl.ds(chunks[number], HALF)
        values = inc[:, view].astype(F32) * scale_in[:, :1]
        normed = (values * gain_ref[:, view].astype(F32)).astype(BF16)
        logits = lax.dot_general(
            normed, router_ref[:, view], (((1,), (1,)), ((), ())), preferred_element_type=F32
        )
        return normed, logits

    def view_a(block, piece):
        return za.at[block, :, pl.ds(piece * QUARTER, QUARTER)]

    def view_b(block, piece):
        return zb.at[block, :, pl.ds(piece * (WIDTH_BX // 2), WIDTH_BX // 2)]

    sent_a, sent_b = [], []
    ring_a = (view_a, 4, za_send, za_recv, sent_a)
    ring_b = (view_b, 2, zb_send, zb_recv, sent_b)

    def gather_copy(kind, way, hop, piece):
        view, _, sends, recvs, _ = kind
        there = view(wrap(local - sign[way] * (hop - 1)), piece)
        return remote(
            there, there, sends.at[way, hop - 1, piece], recvs.at[way, hop - 1, piece], ring[way]
        )

    def gather_open(kind, pieces):
        for piece in pieces:
            for way in range(2):
                start(gather_copy(kind, way, 1, piece), kind[4])

    def gather_step(kind, hop, pieces):
        for piece in pieces:
            for way in range(2):
                hops = hops_of(piece, kind[1], way)
                if hop <= hops:
                    gather_copy(kind, way, hop, piece).wait_recv()
                if hop < hops:
                    start(gather_copy(kind, way, hop + 1, piece), kind[4])

    xa_copies = ([], [])

    def spread(half, normed):
        na[...] = normed

        @pl.loop(0, QUARTER // LANES)
        def _(tile):
            parts = [
                matmul(chosen, na[:, lanes_at(base + tile * LANES, LANES)]).reshape(EXPERTS, CAP, LANES)
                for base in (0, QUARTER)
            ]
            disp[half, :, :, lanes_at(tile * LANES, LANES)] = jnp.concatenate(parts, axis=1).astype(BF16)

        for step in range(1, EXPERTS):
            other = wrap(group + step)
            copy = remote(
                disp.at[half, other], xa.at[half, group],
                xa_send.at[half, step], xa_recv.at[half, step], {"group": other},
            )
            start(copy, xa_copies[half])
        xa[half, group] = disp[half, group]

    def compact(half):
        for copy in xa_copies[half]:
            copy.wait_recv()

        @pl.loop(0, QUARTER // LANES)
        def _(tile):
            rows = xa[half, :, :, lanes_at(tile * LANES, LANES)].astype(F32)
            for quarter in range(2):
                part = rows[:, quarter * CAP : (quarter + 1) * CAP].reshape(SLOTS, LANES).astype(BF16)
                begin = half * HALF + quarter * QUARTER
                za[local, :, lanes_at(begin + tile * LANES, LANES)] = part

        gather_open(ring_a, (2 * half, 2 * half + 1))

    def select(pair, place):
        both = zb[pl.ds(2 * pair, 2), :, :META].reshape(2 * ROWS, META).astype(F32)
        masks = pair_masks(both)
        selector = jnp.transpose((masks[0] | masks[1]).astype(F32)).astype(BF16)

        @pl.loop(0, WIDTH_B // TILE)
        def _(tile):
            rows = zb[pl.ds(2 * pair, 2), :, lanes_at(META + tile * TILE, TILE)].reshape(2 * ROWS, TILE)
            out = matmul(selector, rows).astype(BF16).reshape(EXPERTS, TWICE, TILE)
            xs[place, :, :, lanes_at(tile * TILE, TILE)] = out

    def send_pair(pair, place, sends, recvs):
        copies = []
        for step in range(1, EXPERTS):
            other = wrap(group + step)
            copy = remote(
                xs.at[place, other], xr.at[group, pair_at(pair)], sends.at[step], recvs.at[step],
                {"group": other},
            )
            start(copy, copies)
        xr[group, pair_at(pair)] = xs[place, group]
        return copies

    xb_copies = []

    def give_pair(order):
        if order >= 2:
            for copy in xb_copies[order - 2]:
                copy.wait_send()
        select(pairs[order], order % 2)
        xb_copies.append(send_pair(pairs[order], order % 2, xb_send.at[order], xb_recv.at[order]))

    normed, logits = normed_chunk(0)
    zb[local, :, :META] = meta.astype(BF16)
    zb[local, :, META : META + HALF] = normed
    gather_open(ring_b, (0,))
    normed, more = normed_chunk(1)
    logits = logits + more
    spread(0, normed)
    gather_step(ring_b, 1, (0,))
    normed, more = normed_chunk(2)
    logits = logits + more
    spread(1, normed)
    gather_step(ring_b, 2, (0,))
    normed, more = normed_chunk(3)
    zb[local, :, META + HALF : GATES_AT] = normed
    affinity = jax.nn.sigmoid(logits + more)
    expert = lax.broadcasted_iota(jnp.int32, (ROWS, EXPERTS), 1).astype(F32)
    picked = [
        jnp.sum(jnp.where(experts[choice] == expert, affinity, 0.0), axis=1, keepdims=True)
        for choice in range(2)
    ]
    gates = jnp.zeros((ROWS, META), F32)
    for choice in range(2):
        gate = 2.5 * picked[choice] / (picked[0] + picked[1])
        high = gate.astype(BF16).astype(F32)
        gates = jnp.where(lane == 2 * choice, high, gates)
        gates = jnp.where(lane == 2 * choice + 1, gate - high, gates)
    zb[local, :, GATES_AT:] = gates.astype(BF16)
    gather_open(ring_b, (1,))
    gather_step(ring_b, 3, (0,))
    compact(0)
    gather_step(ring_b, 1, (1,))
    give_pair(0)
    gather_step(ring_b, 4, (0,))
    compact(1)
    gather_step(ring_b, 2, (1,))
    give_pair(1)
    gather_step(ring_b, 3, (1,))
    gather_step(ring_b, 4, (1,))

    def add_a(block):
        block = wrap(block)
        rows = za[block]
        for half, weights in enumerate((wg, wu)):
            out = matmul(rows, weights[:WIDTH_A, :]).reshape(EXPERTS, CAP, HIDDEN)
            hacc[block, :, :, half * HIDDEN : (half + 1) * HIDDEN] = out

    def take(hop):
        count = 1 if hop in (0, 4) else 2

        @pl.loop(0, count)
        def _(i):
            add_a(local - hop + 2 * hop * i)

    def finish(order):
        pair = pairs[order]
        rows = xr[:, pair_at(pair), :].reshape(EXPERTS * TWICE, WIDTH_B)
        parts = []
        for half, weights in enumerate((wg, wu)):
            out = matmul(rows, weights[WIDTH_A:, :]).reshape(EXPERTS, 2, CAP, HIDDEN)
            done = [
                hacc[2 * pair + block, :, :, half * HIDDEN : (half + 1) * HIDDEN] + out[:, block]
                for block in range(2)
            ]
            parts.append(done)
        active = [jax.nn.silu(parts[0][block]) * parts[1][block] for block in range(2)]
        for block in range(2):
            acta[2 * pair + block] = active[block].reshape(SLOTS, HIDDEN).astype(BF16)
        both = jnp.concatenate(active, axis=1)
        actb[pair] = both.reshape(EXPERTS * TWICE, HIDDEN).astype(BF16)
        for step in range(1, EXPERTS):
            pl.semaphore_signal(free_x.at[order], inc=1, device_id={"group": wrap(group + step)})

    def product_b(pair, place):
        @pl.loop(0, WIDTH_B // TILE)
        def _(tile):
            weights = wd[:, lanes_at(WIDTH_A + tile * TILE, TILE)]
            out = matmul(actb[pair], weights).astype(BF16).reshape(EXPERTS, TWICE, TILE)
            xs[place, :, :, lanes_at(tile * TILE, TILE)] = out

    xc_copies = {}

    def return_pair(order, place, blocking):
        for copy in blocking:
            copy.wait_send()
        product_b(pairs[order], place)
        pl.semaphore_wait(free_x.at[order], EXPERTS - 1)
        xc_copies[order] = send_pair(pairs[order], place, xc_send.at[order], xc_recv.at[order])

    loads[0].wait()
    loads[1].wait()
    take(0)
    for hop in range(1, 5):
        gather_step(ring_a, hop, range(4))
        take(hop)
        if hop == 4:
            loads[2].wait()
            for copy in sent_a:
                copy.wait_send()
            for way in range(2):
                pl.semaphore_signal(free_z, inc=1, device_id=ring[way])
        for copy in xb_copies[hop - 1]:
            copy.wait_recv()
        if hop == 4:
            return_pair(0, 0, xb_copies[2])
        finish(hop - 1)
        if hop < 3:
            give_pair(hop + 1)


    sent_c = []

    def product_a(block, piece, fresh):
        block = wrap(block)

        def part(begin, size):
            columns = lanes_at(begin, size)
            out = matmul(acta[block], wd[:, columns])
            if not fresh:
                out = out + za[block, :, columns].astype(F32)
            za[block, :, columns] = out.astype(BF16)

        @pl.loop(0, QUARTER // TILE)
        def _(tile):
            part(piece * QUARTER + tile * TILE, TILE)

        part(piece * QUARTER + QUARTER // TILE * TILE, QUARTER % TILE)

    def sum_copy_a(way, hop, piece):
        block = wrap(local + sign[way] * (5 - hop))
        columns = pl.ds(piece * QUARTER, QUARTER)
        lands = zd.at[:, columns] if (way, hop) == (1, 4) else za.at[block, :, columns]
        return remote(
            za.at[block, :, columns], lands,
            zc_send.at[way, hop - 1, piece], zc_recv.at[way, hop - 1, piece], ring[way],
        )

    def sum_open_a(hop):
        for piece in range(4):
            for way in range(2):
                if hop == 5 - hops_of(piece, 4, way):
                    product_a(local + sign[way] * (5 - hop), piece, True)
                    start(sum_copy_a(way, hop, piece), sent_c)

    def sum_step_a(hop):
        for piece in range(4):
            for way in range(2):
                if hop > 5 - hops_of(piece, 4, way):
                    sum_copy_a(way, hop - 1, piece).wait_recv()
                    product_a(local + sign[way] * (5 - hop), piece, False)
                    start(sum_copy_a(way, hop, piece), sent_c)

    def sum_copy_b(way, hop, piece):
        block = wrap(local + sign[way] * (5 - hop))
        return remote(
            zb.at[block, :, pl.ds(META + piece * HALF, HALF)],
            (tu, td)[way].at[hop - 1, :, pl.ds(piece * HALF, HALF)],
            ze_send.at[way, hop - 1, piece], ze_recv.at[way, hop - 1, piece], ring[way],
        )

    def sum_step_b(hop):
        for piece in range(2):
            for way in range(2):
                opens = 5 - hops_of(piece, 2, way)
                if hop > opens:
                    sum_copy_b(way, hop - 1, piece).wait_recv()
                    block = wrap(local + sign[way] * (5 - hop))
                    came = (tu, td)[way][hop - 2, :, pl.ds(piece * HALF, HALF)]
                    zb[block, :, pl.ds(META + piece * HALF, HALF)] += came
                if hop >= opens:
                    start(sum_copy_b(way, hop, piece), sent_c)

    def mix_pair(order):
        pair = pairs[order]
        for copy in xc_copies[order]:
            copy.wait_recv()
        both = zb[pl.ds(2 * pair, 2), :, :META].reshape(2 * ROWS, META).astype(F32)
        weights = zb[pl.ds(2 * pair, 2), :, GATES_AT:].reshape(2 * ROWS, META).astype(F32)
        high, low = gate_matrices(both, weights)

        @pl.loop(0, WIDTH_B // TILE)
        def _(tile):
            rows = xr[:, pair_at(pair), lanes_at(tile * TILE, TILE)].reshape(EXPERTS * TWICE, TILE)
            mixed = matmul(high, rows) + matmul(low, rows)
            mixed = mixed.astype(BF16).reshape(2, ROWS, TILE)
            zb[pl.ds(2 * pair, 2), :, lanes_at(META + tile * TILE, TILE)] = mixed

    pl.semaphore_wait(free_z, 2)
    sum_open_a(1)
    return_pair(3, 1, xb_copies[3])
    sum_open_a(2)
    for copy in sent_b + xa_copies[0] + xa_copies[1]:
        copy.wait_send()
    sum_step_a(2)
    return_pair(2, 0, xc_copies[0])
    sum_step_a(3)
    return_pair(1, 1, xc_copies[3])
    mix_pair(3)
    sum_step_b(1)
    sum_step_a(4)
    mix_pair(2)
    sum_step_b(2)
    mix_pair(0)

    xe_copies = ([], [])

    def total_a(columns):
        total = matmul(acta[local], wd[:, columns])
        total = total + za[local, :, columns].astype(F32) + zd[:, columns].astype(F32)
        return total.reshape(EXPERTS, CAP, LANES)

    for half in range(2):
        for piece in (2 * half, 2 * half + 1):
            for way in range(2):
                sum_copy_a(way, 4, piece).wait_recv()

        @pl.loop(0, QUARTER // LANES)
        def _(tile, half=half):
            parts = [
                total_a(lanes_at(half * HALF + quarter * QUARTER + tile * LANES, LANES))
                for quarter in range(2)
            ]
            disp[half, :, :, lanes_at(tile * LANES, LANES)] = jnp.concatenate(parts, axis=1).astype(BF16)

        for step in range(1, EXPERTS):
            other = wrap(group + step)
            copy = remote(
                disp.at[half, other], xa.at[half, group],
                xe_send.at[half, step], xe_recv.at[half, step], {"group": other},
            )
            start(copy, xe_copies[half])
        xa[half, group] = disp[half, group]
    mix_pair(1)
    sum_step_b(3)
    sum_step_b(4)

    own, weights = zb[local, :, :META].astype(F32), zb[local, :, GATES_AT:].astype(F32)
    high, low = gate_matrices(
        jnp.concatenate([own, own], axis=0), jnp.concatenate([weights, weights], axis=0)
    )
    for half in range(2):
        for copy in xe_copies[half]:
            copy.wait_recv()

        @pl.loop(0, QUARTER // LANES)
        def _(tile, half=half):
            rows = xa[half, :, :, lanes_at(tile * LANES, LANES)].reshape(EXPERTS * TWICE, LANES)
            mixed = matmul(high, rows) + matmul(low, rows)
            for quarter in range(2):
                columns = lanes_at(half * HALF + quarter * QUARTER + tile * LANES, LANES)
                part = mixed[quarter * ROWS : (quarter + 1) * ROWS]
                out_ref[:, columns] = (inc[:, columns].astype(F32) + part).astype(BF16)

    for piece in range(2):
        for way in range(2):
            sum_copy_b(way, 4, piece).wait_recv()

    @pl.loop(0, WIDTH_B // TILE)
    def _(tile):
        columns = lanes_at(tile * TILE, TILE)
        places = lanes_at(WIDTH_A + tile * TILE, TILE)
        mixed = zb[local, :, lanes_at(META + tile * TILE, TILE)].astype(F32)
        mixed = mixed + tu[3, :, columns].astype(F32) + td[3, :, columns].astype(F32)
        out_ref[:, places] = (inc[:, places].astype(F32) + mixed).astype(BF16)

    scale_copy.wait_send()
    for copy in shifts[2:] + sent_c + xe_copies[0] + xe_copies[1] + xc_copies[2] + xc_copies[1]:
        copy.wait_send()


def whole(*shape, dtype=BF16):
    return pltpu.VMEM(shape, dtype)


def dma(*shape):
    return pltpu.SemaphoreType.DMA(shape)


def per_device(hidden_in, norm_gain, router, w_gate, w_up, w_down, routes):
    vmem = pl.BlockSpec(memory_space=pltpu.VMEM)
    anywhere = pl.BlockSpec(memory_space=pl.ANY)
    out = pl.pallas_call(
        layer_kernel,
        out_shape=jax.ShapeDtypeStruct((ROWS, WIDTH), BF16),
        in_specs=[vmem] * 4 + [anywhere] * 3,
        out_specs=vmem,
        scratch_shapes=[
            whole(WIDTH, HIDDEN),
            whole(WIDTH, HIDDEN),
            whole(HIDDEN, WIDTH),
            whole(ROWS, WIDTH),
            whole(ROWS, LANES, dtype=F32),
            whole(ROWS, LANES, dtype=F32),
            whole(ROWS, HALF),
            whole(2, EXPERTS, TWICE, QUARTER),
            whole(2, EXPERTS, TWICE, QUARTER),
            whole(LOCALS, SLOTS, WIDTH_A),
            whole(SLOTS, WIDTH_A),
            whole(LOCALS, ROWS, WIDTH_BX),
            whole(2, EXPERTS, TWICE, WIDTH_B),
            whole(EXPERTS, SLOTS, WIDTH_B),
            whole(LOCALS, EXPERTS, CAP, 2 * HIDDEN, dtype=F32),
            whole(LOCALS, SLOTS, HIDDEN),
            whole(PAIRS, EXPERTS * TWICE, HIDDEN),
            whole(4, ROWS, WIDTH_B),
            whole(4, ROWS, WIDTH_B),
            dma(3), dma(5), dma(5), dma(2, 8), dma(2, 8), dma(2, 4, 2), dma(2, 4, 2),
            dma(2, 4, 4), dma(2, 4, 4), dma(4, 8), dma(4, 8),
            pltpu.SemaphoreType.REGULAR((4,)), pltpu.SemaphoreType.REGULAR,
            dma(4, 8), dma(4, 8), dma(2, 4, 4), dma(2, 4, 4), dma(2, 4, 2), dma(2, 4, 2),
            dma(2, 8), dma(2, 8),
        ],
        compiler_params=pltpu.CompilerParams(
            collective_id=0, has_side_effects=True, vmem_limit_bytes=VMEM_BYTES
        ),
        name="layer",
    )(hidden_in[0], norm_gain, router[0].T, routes[0].T, w_gate[0, 0], w_up[0, 0], w_down[0, 0])
    return out[None]


def solution(mesh):
    placed = (
        P("section", ("group", "local"), None),
        P("section", None),
        P("section", None, None),
        P("section", "group", None, "local"),
        P("section", "group", None, "local"),
        P("section", "group", "local", None),
        P("section", ("group", "local"), None),
    )
    return jax.shard_map(
        per_device,
        mesh=mesh,
        in_specs=placed,
        out_specs=P("section", ("group", "local"), None),
        check_vma=False,
    )
```

time: 1100 us -> 323 us (0.29); the launches traced: 1080 us -> 323 us
  waiting for transfers between devices: 510 us -> 0 us
  blocking collectives: 492 us -> 0 us
  Pallas kernels: 0 us -> 321 us
  matrix products: 32.7 us -> 0 us
  other arithmetic: 22.4 us -> 0 us
  local copies, waits for them, and re-layouts: 13.3 us -> 2.16 us
    all_to_all x1 -> x0, waiting for transfers between devices: 492 us -> none  [per_device(): lax.all_to_all(partial_value, ('group', 'local'), split_axis=0, concat_ax...]
    all_to_all x1 -> x0, blocking collectives: 492 us -> none  [per_device(): lax.all_to_all(copies, ('group', 'local'), split_axis=0, concat_axis=0, t...]
    pallas_call x0 -> x1, Pallas kernels: none -> 321 us  [per_device(): pl.pallas_call(layer_kernel, out_shape=jax.ShapeDtypeStruct((ROWS, WIDTH)...]
    dot_general x5 -> x0, matrix products: 32.7 us -> none  [the longest x1 12.7 us: per_device(): jnp.dot(active, down_matrix, preferred_element_type=jnp.float32)]
    reduce_sum x5 -> x0, other arithmetic: 20.1 us -> none  [the longest x1 12.4 us: per_device(): jnp.sum(came_back.reshape(group_count, local_count, capacity, width).asty...]
    ppermute x1 -> x0, waiting for transfers between devices: 17.2 us -> none  [from_behind(): lax.ppermute(shard, axis, [(i, (i + by) % count) for i in range(count)])]
  transfers between devices with their start and end apart: 2 -> 0, of which waited for: 2 -> 0; matrix products, arithmetic and copies ran while one was open for 0% -> 0% of each run, Pallas kernels for 0% -> 0%
where the time goes in v3:
time: 323 us
  Pallas kernels  321 us (99%)
    pallas_call x1, Pallas kernels, per_device(): pl.pallas_call(layer_kernel, out_shape=jax.ShapeDtypeStruct((ROWS, WIDTH)...  321 us

profile of v3, /device:TPU:1, one launch (start us, length us, event | category | flops | bytes accessed | tf_op | source)
XLA Modules:
  0.0 323.3 jit_solution(11521048727784774690)
XLA Ops:
  0.0 321.1 %layer.1 = bf16[64,7168]{1,0:T(8,128)(2,1)} custom-call(bf16[64,7168]{1,0:T(8,128)(2,1)} %bitcast.15, bf16[1,7168]{1,0:T(2,128)(2,1)} %gain_ref.1, bf16[8,7168]{1,0:T(8,128)(2,1)} %bitcast.16, s32[2,64]{1,0:T(2,128)} %bitcast.17, bf16[7168,256]{1,0:T(8,128)(2,1)} %bitcast.11, bf16[7168,256]{1,0:T(8,128)(2,1)} %bitcast.12, bf16[256,7168]{1,0:T(8,128)(2,1)} %bitcast.13), custom_call_target="tpu_custom_call" | custom-call | tf_op jit(solution)/shard_map/layer/pallas_call | solution.py:561
  321.1 2.2 copy.9

commit v4 on v3

--- a/solution.py
+++ b/solution.py
@@ -8,11 +8,11 @@
 WIDTH = 7168
 WIDTH_A = 3584
 WIDTH_B = WIDTH - WIDTH_A
-HALF = 1792
+META = 128
 QUARTER = 896
-META = 128
-WIDTH_BX = META + WIDTH_B + META
-GATES_AT = META + WIDTH_B
+QUARTERS = ((0, 896), (896, 896), (1792, 896), (2688, 896))
+PARTS = ((0, 1792), (1792, WIDTH_B - 1792))
+WIDTH_BX = META + WIDTH_B
 EXPERTS = 8
 LOCALS = 8
 SECTIONS = 4
@@ -42,6 +42,15 @@
     return pl.ds(pl.multiple_of(start, LANES), size)
 
 
+def sweep(width, part):
+    @pl.loop(0, width // TILE)
+    def _(tile):
+        part(tile * TILE, TILE)
+
+    if width % TILE:
+        part(width // TILE * TILE, width % TILE)
+
+
 def pair_at(pair):
     return pl.ds(pl.multiple_of(pair * TWICE, TWICE), TWICE)
 
@@ -50,6 +59,15 @@
     return pltpu.make_async_remote_copy(
         src_ref=src, dst_ref=dst, send_sem=send, recv_sem=recv, device_id=device
     )
+
+
+def peers_of(group):
+    chip, core = group // 2, lax.rem(group, 2)
+    out = []
+    for index, (ahead, flip) in enumerate(((1, 0), (3, 0), (2, 0), (1, 1), (3, 1), (2, 1), (0, 1))):
+        there = 1 - core if flip else core
+        out.append((index, wrap(chip + ahead, 4) * 2 + there))
+    return out
 
 
 def hops_of(piece, pieces, way):
@@ -92,9 +110,9 @@
 
 def layer_kernel(
     hid_ref, gain_ref, router_ref, routes_ref, wg_hbm, wu_hbm, wd_hbm, out_ref,
-    wg, wu, wd, inc, scale_out, scale_in, na, disp, xa, za, zd, zb, xs, xr, hacc, acta, actb, tu, td,
-    w_sem, y_send, y_recv, xa_send, xa_recv, zb_send, zb_recv, za_send, za_recv, xb_send, xb_recv,
-    free_x, free_z,
+    wg, wu, wd, inc, scale_out, scale_in, na, disp, xa, za, zd, zb, zg, xs, xr, hacc, acta, actb, tu, td,
+    w_sem, y_send, y_recv, xa_send, xa_recv, zb_send, zb_recv, zg_send, zg_recv, za_send, za_recv,
+    xb_send, xb_recv, free_x, free_z,
     xc_send, xc_recv, zc_send, zc_recv, ze_send, ze_recv, xe_send, xe_recv,
 ):
     section = lax.axis_index("section")
@@ -103,20 +121,20 @@
     after = {"section": wrap(section + 1, SECTIONS)}
     sign = (1, -1)
     pairs = pairs_near_first(local)
+    peers = peers_of(group)
 
     barrier = pltpu.get_barrier_semaphore()
     pl.semaphore_signal(barrier, inc=1, device_id={"section": wrap(section - 1, SECTIONS)})
     for way in range(2):
         pl.semaphore_signal(barrier, inc=1, device_id=ring[way])
-    for step in range(1, EXPERTS):
-        pl.semaphore_signal(barrier, inc=1, device_id={"group": wrap(group + step)})
+    for _, other in peers:
+        pl.semaphore_signal(barrier, inc=1, device_id={"group": other})
     loads = [
         pltpu.make_async_copy(hbm, here, w_sem.at[i])
         for i, (hbm, here) in enumerate(((wg_hbm, wg), (wu_hbm, wu), (wd_hbm, wd)))
     ]
     for load in loads:
         load.start()
-    pl.semaphore_wait(barrier, 1 + 2 + EXPERTS - 1)
 
     def start(copy, into):
         copy.start()
@@ -124,21 +142,23 @@
         return copy
 
 
-    chunks = (WIDTH_A, 0, HALF, WIDTH_A + HALF)
+    chunks = tuple((WIDTH_A + begin, size) for begin, size in PARTS)
+    chunks += ((0, 2 * QUARTER), (2 * QUARTER, WIDTH_A - 2 * QUARTER))
     shifts = []
-    for number, begin in enumerate(chunks):
-        view = pl.ds(begin, HALF)
+    for number, (begin, size) in enumerate(chunks):
+        view = pl.ds(begin, size)
         shifts.append(
             remote(hid_ref.at[:, view], inc.at[:, view], y_send.at[number], y_recv.at[number], after)
         )
-    shifts[0].start()
     squares = jnp.zeros((ROWS, 1), F32)
-    for begin in chunks:
-        values = hid_ref[:, pl.ds(begin, HALF)].astype(F32)
+    for begin, size in chunks:
+        values = hid_ref[:, pl.ds(begin, size)].astype(F32)
         squares = squares + jnp.sum(values * values, axis=-1, keepdims=True)
     scale_out[...] = jnp.broadcast_to(lax.rsqrt(squares / WIDTH + 1e-06), (ROWS, LANES))
     scale_copy = remote(scale_out, scale_in, y_send.at[4], y_recv.at[4], after)
+    pl.semaphore_wait(barrier, 1 + 2 + EXPERTS - 1)
     scale_copy.start()
+    shifts[0].start()
     shifts[1].start()
 
     square = (ROWS, ROWS)
@@ -171,7 +191,7 @@
             shifts[number + 2].start()
         if number == 0:
             scale_copy.wait_recv()
-        view = pl.ds(chunks[number], HALF)
+        view = pl.ds(*chunks[number])
         values = inc[:, view].astype(F32) * scale_in[:, :1]
         normed = (values * gain_ref[:, view].astype(F32)).astype(BF16)
         logits = lax.dot_general(
@@ -180,14 +200,19 @@
         return normed, logits
 
     def view_a(block, piece):
-        return za.at[block, :, pl.ds(piece * QUARTER, QUARTER)]
+        return za.at[block, :, pl.ds(*QUARTERS[piece])]
 
     def view_b(block, piece):
-        return zb.at[block, :, pl.ds(piece * (WIDTH_BX // 2), WIDTH_BX // 2)]
+        begin, size = PARTS[piece]
+        return zb.at[block, :, pl.ds(META + begin, size) if piece else pl.ds(0, META + size)]
+
+    def view_g(block, piece):
+        return zg.at[block]
 
     sent_a, sent_b = [], []
     ring_a = (view_a, 4, za_send, za_recv, sent_a)
     ring_b = (view_b, 2, zb_send, zb_recv, sent_b)
+    ring_g = (view_g, 2, zg_send, zg_recv, sent_b)
 
     def gather_copy(kind, way, hop, piece):
         view, _, sends, recvs, _ = kind
@@ -212,86 +237,112 @@
 
     xa_copies = ([], [])
 
+    def by_quarters(half, part):
+        few = QUARTERS[2 * half + 1][1] // LANES
+
+        @pl.loop(0, few)
+        def _(tile):
+            part(tile * LANES, 2)
+
+        if few * LANES < QUARTER:
+            part(few * LANES, 1)
+
+    def stacked(parts):
+        if len(parts) == 1:
+            parts = parts + [jnp.zeros_like(parts[0])]
+        return jnp.concatenate(parts, axis=1).astype(BF16)
+
+    def exchange(half, sends, recvs, copies):
+        for step, other in peers:
+            copy = remote(
+                disp.at[half, other], xa.at[half, group], sends.at[half, step], recvs.at[half, step],
+                {"group": other},
+            )
+            start(copy, copies)
+        xa[half, group] = disp[half, group]
+
     def spread(half, normed):
-        na[...] = normed
-
-        @pl.loop(0, QUARTER // LANES)
-        def _(tile):
+        na[:, : normed.shape[1]] = normed
+
+        def part(begin, quarters):
             parts = [
-                matmul(chosen, na[:, lanes_at(base + tile * LANES, LANES)]).reshape(EXPERTS, CAP, LANES)
-                for base in (0, QUARTER)
+                matmul(chosen, na[:, lanes_at(quarter * QUARTER + begin, LANES)])
+                for quarter in range(quarters)
             ]
-            disp[half, :, :, lanes_at(tile * LANES, LANES)] = jnp.concatenate(parts, axis=1).astype(BF16)
-
-        for step in range(1, EXPERTS):
-            other = wrap(group + step)
-            copy = remote(
-                disp.at[half, other], xa.at[half, group],
-                xa_send.at[half, step], xa_recv.at[half, step], {"group": other},
-            )
-            start(copy, xa_copies[half])
-        xa[half, group] = disp[half, group]
+            parts = [rows.reshape(EXPERTS, CAP, LANES) for rows in parts]
+            disp[half, :, :, lanes_at(begin, LANES)] = stacked(parts)
+
+        by_quarters(half, part)
+        exchange(half, xa_send, xa_recv, xa_copies[half])
 
     def compact(half):
         for copy in xa_copies[half]:
             copy.wait_recv()
 
-        @pl.loop(0, QUARTER // LANES)
-        def _(tile):
-            rows = xa[half, :, :, lanes_at(tile * LANES, LANES)].astype(F32)
-            for quarter in range(2):
-                part = rows[:, quarter * CAP : (quarter + 1) * CAP].reshape(SLOTS, LANES).astype(BF16)
-                begin = half * HALF + quarter * QUARTER
-                za[local, :, lanes_at(begin + tile * LANES, LANES)] = part
-
+        def part(begin, quarters):
+            rows = xa[half, :, :, lanes_at(begin, LANES)].astype(F32)
+            for quarter in range(quarters):
+                some = rows[:, quarter * CAP : (quarter + 1) * CAP].reshape(SLOTS, LANES)
+                columns = lanes_at((2 * half + quarter) * QUARTER + begin, LANES)
+                za[local, :, columns] = some.astype(BF16)
+
+        by_quarters(half, part)
         gather_open(ring_a, (2 * half, 2 * half + 1))
 
-    def select(pair, place):
+    def select(pair, place, begin, width):
         both = zb[pl.ds(2 * pair, 2), :, :META].reshape(2 * ROWS, META).astype(F32)
         masks = pair_masks(both)
         selector = jnp.transpose((masks[0] | masks[1]).astype(F32)).astype(BF16)
 
-        @pl.loop(0, WIDTH_B // TILE)
-        def _(tile):
-            rows = zb[pl.ds(2 * pair, 2), :, lanes_at(META + tile * TILE, TILE)].reshape(2 * ROWS, TILE)
-            out = matmul(selector, rows).astype(BF16).reshape(EXPERTS, TWICE, TILE)
-            xs[place, :, :, lanes_at(tile * TILE, TILE)] = out
-
-    def send_pair(pair, place, sends, recvs):
+        def part(start, size):
+            rows = zb[pl.ds(2 * pair, 2), :, lanes_at(META + begin + start, size)]
+            out = matmul(selector, rows.reshape(2 * ROWS, size)).astype(BF16)
+            xs[place, :, :, lanes_at(begin + start, size)] = out.reshape(EXPERTS, TWICE, size)
+
+        sweep(width, part)
+
+    def send_pair(pair, place, sends, recvs, begin=0, width=WIDTH_B):
         copies = []
-        for step in range(1, EXPERTS):
-            other = wrap(group + step)
+        columns = pl.ds(begin, width)
+        for step, other in peers:
             copy = remote(
-                xs.at[place, other], xr.at[group, pair_at(pair)], sends.at[step], recvs.at[step],
-                {"group": other},
+                xs.at[place, other, :, columns], xr.at[group, pair_at(pair), columns],
+                sends.at[step], recvs.at[step], {"group": other},
             )
             start(copy, copies)
-        xr[group, pair_at(pair)] = xs[place, group]
+        xr[group, pair_at(pair), columns] = xs[place, group, :, columns]
         return copies
 
-    xb_copies = []
-
-    def give_pair(order):
-        if order >= 2:
-            for copy in xb_copies[order - 2]:
+    xb_copies = [[], [], [], []]
+
+    def give_pair(order, begin=0, width=WIDTH_B):
+        if order == 3:
+            for copy in xb_copies[0]:
                 copy.wait_send()
-        select(pairs[order], order % 2)
-        xb_copies.append(send_pair(pairs[order], order % 2, xb_send.at[order], xb_recv.at[order]))
+        select(pairs[order], order % 3, begin, width)
+        row = order if begin == 0 else 4
+        xb_copies[order] += send_pair(
+            pairs[order], order % 3, xb_send.at[row], xb_recv.at[row], begin, width
+        )
 
     normed, logits = normed_chunk(0)
     zb[local, :, :META] = meta.astype(BF16)
-    zb[local, :, META : META + HALF] = normed
+    zb[local, :, META : META + PARTS[1][0]] = normed
     gather_open(ring_b, (0,))
     normed, more = normed_chunk(1)
     logits = logits + more
-    spread(0, normed)
+    zb[local, :, META + PARTS[1][0] :] = normed
+    gather_open(ring_b, (1,))
     gather_step(ring_b, 1, (0,))
+    give_pair(0, *PARTS[0])
     normed, more = normed_chunk(2)
     logits = logits + more
-    spread(1, normed)
+    spread(0, normed)
+    gather_step(ring_b, 1, (1,))
+    give_pair(0, *PARTS[1])
     gather_step(ring_b, 2, (0,))
     normed, more = normed_chunk(3)
-    zb[local, :, META + HALF : GATES_AT] = normed
+    spread(1, normed)
     affinity = jax.nn.sigmoid(logits + more)
     expert = lax.broadcasted_iota(jnp.int32, (ROWS, EXPERTS), 1).astype(F32)
     picked = [
@@ -304,18 +355,18 @@
         high = gate.astype(BF16).astype(F32)
         gates = jnp.where(lane == 2 * choice, high, gates)
         gates = jnp.where(lane == 2 * choice + 1, gate - high, gates)
-    zb[local, :, GATES_AT:] = gates.astype(BF16)
-    gather_open(ring_b, (1,))
+    zg[local] = gates.astype(BF16)
+    gather_open(ring_g, (0,))
+    gather_step(ring_b, 2, (1,))
+    give_pair(1)
     gather_step(ring_b, 3, (0,))
     compact(0)
-    gather_step(ring_b, 1, (1,))
-    give_pair(0)
+    gather_step(ring_b, 3, (1,))
+    compact(1)
+    give_pair(2)
     gather_step(ring_b, 4, (0,))
-    compact(1)
-    gather_step(ring_b, 2, (1,))
-    give_pair(1)
-    gather_step(ring_b, 3, (1,))
     gather_step(ring_b, 4, (1,))
+    gather_step(ring_g, 1, (0,))
 
     def add_a(block):
         block = wrap(block)
@@ -347,30 +398,38 @@
             acta[2 * pair + block] = active[block].reshape(SLOTS, HIDDEN).astype(BF16)
         both = jnp.concatenate(active, axis=1)
         actb[pair] = both.reshape(EXPERTS * TWICE, HIDDEN).astype(BF16)
-        for step in range(1, EXPERTS):
-            pl.semaphore_signal(free_x.at[order], inc=1, device_id={"group": wrap(group + step)})
+        for _, other in peers:
+            pl.semaphore_signal(free_x.at[order], inc=1, device_id={"group": other})
 
     def product_b(pair, place):
-        @pl.loop(0, WIDTH_B // TILE)
-        def _(tile):
-            weights = wd[:, lanes_at(WIDTH_A + tile * TILE, TILE)]
-            out = matmul(actb[pair], weights).astype(BF16).reshape(EXPERTS, TWICE, TILE)
-            xs[place, :, :, lanes_at(tile * TILE, TILE)] = out
+        def part(begin, size):
+            out = matmul(actb[pair], wd[:, lanes_at(WIDTH_A + begin, size)]).astype(BF16)
+            xs[place, :, :, lanes_at(begin, size)] = out.reshape(EXPERTS, TWICE, size)
+
+        sweep(WIDTH_B, part)
 
     xc_copies = {}
 
-    def return_pair(order, place, blocking):
+    def return_pair(order, place, blocking, parts=((0, WIDTH_B),)):
         for copy in blocking:
             copy.wait_send()
         product_b(pairs[order], place)
         pl.semaphore_wait(free_x.at[order], EXPERTS - 1)
-        xc_copies[order] = send_pair(pairs[order], place, xc_send.at[order], xc_recv.at[order])
+        xc_copies[order] = []
+        for number, (begin, width) in enumerate(parts):
+            row = 4 if number else order
+            copies = send_pair(
+                pairs[order], place, xc_send.at[row], xc_recv.at[row], begin, width
+            )
+            xc_copies[order].append(copies)
 
     loads[0].wait()
     loads[1].wait()
     take(0)
     for hop in range(1, 5):
         gather_step(ring_a, hop, range(4))
+        if hop < 4:
+            gather_step(ring_g, hop + 1, (0,))
         take(hop)
         if hop == 4:
             loads[2].wait()
@@ -381,10 +440,10 @@
         for copy in xb_copies[hop - 1]:
             copy.wait_recv()
         if hop == 4:
-            return_pair(0, 0, xb_copies[2])
+            return_pair(1, 1, xb_copies[1])
         finish(hop - 1)
-        if hop < 3:
-            give_pair(hop + 1)
+        if hop == 1:
+            give_pair(3)
 
 
     sent_c = []
@@ -392,22 +451,20 @@
     def product_a(block, piece, fresh):
         block = wrap(block)
 
+        base, width = QUARTERS[piece]
+
         def part(begin, size):
-            columns = lanes_at(begin, size)
+            columns = lanes_at(base + begin, size)
             out = matmul(acta[block], wd[:, columns])
             if not fresh:
                 out = out + za[block, :, columns].astype(F32)
             za[block, :, columns] = out.astype(BF16)
 
-        @pl.loop(0, QUARTER // TILE)
-        def _(tile):
-            part(piece * QUARTER + tile * TILE, TILE)
-
-        part(piece * QUARTER + QUARTER // TILE * TILE, QUARTER % TILE)
+        sweep(width, part)
 
     def sum_copy_a(way, hop, piece):
         block = wrap(local + sign[way] * (5 - hop))
-        columns = pl.ds(piece * QUARTER, QUARTER)
+        columns = pl.ds(*QUARTERS[piece])
         lands = zd.at[:, columns] if (way, hop) == (1, 4) else za.at[block, :, columns]
         return remote(
             za.at[block, :, columns], lands,
@@ -431,55 +488,58 @@
 
     def sum_copy_b(way, hop, piece):
         block = wrap(local + sign[way] * (5 - hop))
+        begin, size = PARTS[piece]
         return remote(
-            zb.at[block, :, pl.ds(META + piece * HALF, HALF)],
-            (tu, td)[way].at[hop - 1, :, pl.ds(piece * HALF, HALF)],
+            zb.at[block, :, pl.ds(META + begin, size)],
+            (tu, td)[way].at[hop - 1, :, pl.ds(begin, size)],
             ze_send.at[way, hop - 1, piece], ze_recv.at[way, hop - 1, piece], ring[way],
         )
 
-    def sum_step_b(hop):
-        for piece in range(2):
+    def sum_step_b(hop, pieces=(0, 1)):
+        for piece in pieces:
             for way in range(2):
                 opens = 5 - hops_of(piece, 2, way)
                 if hop > opens:
                     sum_copy_b(way, hop - 1, piece).wait_recv()
                     block = wrap(local + sign[way] * (5 - hop))
-                    came = (tu, td)[way][hop - 2, :, pl.ds(piece * HALF, HALF)]
-                    zb[block, :, pl.ds(META + piece * HALF, HALF)] += came
+                    begin, size = PARTS[piece]
+                    came = (tu, td)[way][hop - 2, :, pl.ds(begin, size)]
+                    zb[block, :, pl.ds(META + begin, size)] += came
                 if hop >= opens:
                     start(sum_copy_b(way, hop, piece), sent_c)
 
-    def mix_pair(order):
+    def mix_pair(order, number=0, base=0, width=WIDTH_B):
         pair = pairs[order]
-        for copy in xc_copies[order]:
+        for copy in xc_copies[order][number]:
             copy.wait_recv()
         both = zb[pl.ds(2 * pair, 2), :, :META].reshape(2 * ROWS, META).astype(F32)
-        weights = zb[pl.ds(2 * pair, 2), :, GATES_AT:].reshape(2 * ROWS, META).astype(F32)
+        weights = zg[pl.ds(2 * pair, 2)].reshape(2 * ROWS, META).astype(F32)
         high, low = gate_matrices(both, weights)
 
-        @pl.loop(0, WIDTH_B // TILE)
-        def _(tile):
-            rows = xr[:, pair_at(pair), lanes_at(tile * TILE, TILE)].reshape(EXPERTS * TWICE, TILE)
+        def part(begin, size):
+            rows = xr[:, pair_at(pair), lanes_at(base + begin, size)].reshape(EXPERTS * TWICE, size)
             mixed = matmul(high, rows) + matmul(low, rows)
-            mixed = mixed.astype(BF16).reshape(2, ROWS, TILE)
-            zb[pl.ds(2 * pair, 2), :, lanes_at(META + tile * TILE, TILE)] = mixed
+            mixed = mixed.astype(BF16).reshape(2, ROWS, size)
+            zb[pl.ds(2 * pair, 2), :, lanes_at(META + base + begin, size)] = mixed
+
+        sweep(width, part)
 
     pl.semaphore_wait(free_z, 2)
     sum_open_a(1)
-    return_pair(3, 1, xb_copies[3])
+    return_pair(3, 2, xb_copies[2])
     sum_open_a(2)
     for copy in sent_b + xa_copies[0] + xa_copies[1]:
         copy.wait_send()
     sum_step_a(2)
-    return_pair(2, 0, xc_copies[0])
+    return_pair(2, 0, xb_copies[3])
     sum_step_a(3)
-    return_pair(1, 1, xc_copies[3])
+    return_pair(0, 1, xc_copies[1][0], PARTS)
     mix_pair(3)
     sum_step_b(1)
     sum_step_a(4)
     mix_pair(2)
     sum_step_b(2)
-    mix_pair(0)
+    mix_pair(1)
 
     xe_copies = ([], [])
 
@@ -493,27 +553,21 @@
             for way in range(2):
                 sum_copy_a(way, 4, piece).wait_recv()
 
-        @pl.loop(0, QUARTER // LANES)
-        def _(tile, half=half):
+        def part(begin, quarters, half=half):
             parts = [
-                total_a(lanes_at(half * HALF + quarter * QUARTER + tile * LANES, LANES))
-                for quarter in range(2)
+                total_a(lanes_at((2 * half + quarter) * QUARTER + begin, LANES))
+                for quarter in range(quarters)
             ]
-            disp[half, :, :, lanes_at(tile * LANES, LANES)] = jnp.concatenate(parts, axis=1).astype(BF16)
-
-        for step in range(1, EXPERTS):
-            other = wrap(group + step)
-            copy = remote(
-                disp.at[half, other], xa.at[half, group],
-                xe_send.at[half, step], xe_recv.at[half, step], {"group": other},
-            )
-            start(copy, xe_copies[half])
-        xa[half, group] = disp[half, group]
-    mix_pair(1)
+            disp[half, :, :, lanes_at(begin, LANES)] = stacked(parts)
+
+        by_quarters(half, part)
+        exchange(half, xe_send, xe_recv, xe_copies[half])
     sum_step_b(3)
-    sum_step_b(4)
-
-    own, weights = zb[local, :, :META].astype(F32), zb[local, :, GATES_AT:].astype(F32)
+    for piece in range(2):
+        mix_pair(0, piece, *PARTS[piece])
+        sum_step_b(4, (piece,))
+
+    own, weights = zb[local, :, :META].astype(F32), zg[local].astype(F32)
     high, low = gate_matrices(
         jnp.concatenate([own, own], axis=0), jnp.concatenate([weights, weights], axis=0)
     )
@@ -521,30 +575,33 @@
         for copy in xe_copies[half]:
             copy.wait_recv()
 
-        @pl.loop(0, QUARTER // LANES)
-        def _(tile, half=half):
-            rows = xa[half, :, :, lanes_at(tile * LANES, LANES)].reshape(EXPERTS * TWICE, LANES)
+        def part(begin, quarters, half=half):
+            rows = xa[half, :, :, lanes_at(begin, LANES)].reshape(EXPERTS * TWICE, LANES)
             mixed = matmul(high, rows) + matmul(low, rows)
-            for quarter in range(2):
-                columns = lanes_at(half * HALF + quarter * QUARTER + tile * LANES, LANES)
-                part = mixed[quarter * ROWS : (quarter + 1) * ROWS]
-                out_ref[:, columns] = (inc[:, columns].astype(F32) + part).astype(BF16)
+            for quarter in range(quarters):
+                columns = lanes_at((2 * half + quarter) * QUARTER + begin, LANES)
+                some = mixed[quarter * ROWS : (quarter + 1) * ROWS]
+                out_ref[:, columns] = (inc[:, columns].astype(F32) + some).astype(BF16)
+
+        by_quarters(half, part)
 
     for piece in range(2):
         for way in range(2):
             sum_copy_b(way, 4, piece).wait_recv()
 
-    @pl.loop(0, WIDTH_B // TILE)
-    def _(tile):
-        columns = lanes_at(tile * TILE, TILE)
-        places = lanes_at(WIDTH_A + tile * TILE, TILE)
-        mixed = zb[local, :, lanes_at(META + tile * TILE, TILE)].astype(F32)
+    def close(begin, size):
+        columns, places = lanes_at(begin, size), lanes_at(WIDTH_A + begin, size)
+        mixed = zb[local, :, lanes_at(META + begin, size)].astype(F32)
         mixed = mixed + tu[3, :, columns].astype(F32) + td[3, :, columns].astype(F32)
         out_ref[:, places] = (inc[:, places].astype(F32) + mixed).astype(BF16)
 
+    sweep(WIDTH_B, close)
     scale_copy.wait_send()
-    for copy in shifts[2:] + sent_c + xe_copies[0] + xe_copies[1] + xc_copies[2] + xc_copies[1]:
+    for copy in shifts[2:] + sent_c + xe_copies[0] + xe_copies[1]:
         copy.wait_send()
+    for copies in xc_copies[3] + xc_copies[2] + xc_copies[0]:
+        for copy in copies:
+            copy.wait_send()
 
 
 def whole(*shape, dtype=BF16):
@@ -570,13 +627,14 @@
             whole(ROWS, WIDTH),
             whole(ROWS, LANES, dtype=F32),
             whole(ROWS, LANES, dtype=F32),
-            whole(ROWS, HALF),
+            whole(ROWS, 2 * QUARTER),
             whole(2, EXPERTS, TWICE, QUARTER),
             whole(2, EXPERTS, TWICE, QUARTER),
             whole(LOCALS, SLOTS, WIDTH_A),
             whole(SLOTS, WIDTH_A),
             whole(LOCALS, ROWS, WIDTH_BX),
-            whole(2, EXPERTS, TWICE, WIDTH_B),
+            whole(LOCALS, ROWS, META),
+            whole(3, EXPERTS, TWICE, WIDTH_B),
             whole(EXPERTS, SLOTS, WIDTH_B),
             whole(LOCALS, EXPERTS, CAP, 2 * HIDDEN, dtype=F32),
             whole(LOCALS, SLOTS, HIDDEN),
@@ -584,9 +642,9 @@
             whole(4, ROWS, WIDTH_B),
             whole(4, ROWS, WIDTH_B),
             dma(3), dma(5), dma(5), dma(2, 8), dma(2, 8), dma(2, 4, 2), dma(2, 4, 2),
-            dma(2, 4, 4), dma(2, 4, 4), dma(4, 8), dma(4, 8),
+            dma(2, 4, 1), dma(2, 4, 1), dma(2, 4, 4), dma(2, 4, 4), dma(5, 8), dma(5, 8),
             pltpu.SemaphoreType.REGULAR((4,)), pltpu.SemaphoreType.REGULAR,
-            dma(4, 8), dma(4, 8), dma(2, 4, 4), dma(2, 4, 4), dma(2, 4, 2), dma(2, 4, 2),
+            dma(5, 8), dma(5, 8), dma(2, 4, 4), dma(2, 4, 4), dma(2, 4, 2), dma(2, 4, 2),
             dma(2, 8), dma(2, 8),
         ],
         compiler_params=pltpu.CompilerParams(

time: 323 us -> 317 us (0.981)
  Pallas kernels: 321 us -> 315 us
    pallas_call x1, Pallas kernels: 321 us -> 315 us  [per_device(): pl.pallas_call(layer_kernel, out_shape=jax.ShapeDtypeStruct((ROWS, WIDTH)...]
where the time goes in v4:
time: 317 us
  Pallas kernels  315 us (99%)
    pallas_call x1, Pallas kernels, per_device(): pl.pallas_call(layer_kernel, out_shape=jax.ShapeDtypeStruct((ROWS, WIDTH)...  315 us

profile of v4, /device:TPU:1, one launch (start us, length us, event | category | flops | bytes accessed | tf_op | source)
XLA Modules:
  0.0 317.3 jit_solution(2529757601140351043)
XLA Ops:
  0.0 315.1 %layer.1 = bf16[64,7168]{1,0:T(8,128)(2,1)} custom-call(bf16[64,7168]{1,0:T(8,128)(2,1)} %bitcast.15, bf16[1,7168]{1,0:T(2,128)(2,1)} %gain_ref.1, bf16[8,7168]{1,0:T(8,128)(2,1)} %bitcast.16, s32[2,64]{1,0:T(2,128)} %bitcast.17, bf16[7168,256]{1,0:T(8,128)(2,1)} %bitcast.11, bf16[7168,256]{1,0:T(8,128)(2,1)} %bitcast.12, bf16[256,7168]{1,0:T(8,128)(2,1)} %bitcast.13), custom_call_target="tpu_custom_call" | custom-call | tf_op jit(solution)/shard_map/layer/pallas_call | solution.py:618
  315.1 2.2 copy.9

commit v5 on v4

--- a/solution.py
+++ b/solution.py
@@ -6,11 +6,11 @@
 from jax.sharding import PartitionSpec as P
 
 WIDTH = 7168
-WIDTH_A = 3584
+WIDTH_A = 3456
 WIDTH_B = WIDTH - WIDTH_A
 META = 128
 QUARTER = 896
-QUARTERS = ((0, 896), (896, 896), (1792, 896), (2688, 896))
+QUARTERS = ((0, 896), (896, 896), (1792, 896), (2688, 768))
 PARTS = ((0, 1792), (1792, WIDTH_B - 1792))
 WIDTH_BX = META + WIDTH_B
 EXPERTS = 8
@@ -411,9 +411,10 @@
     xc_copies = {}
 
     def return_pair(order, place, blocking, parts=((0, WIDTH_B),)):
-        for copy in blocking:
-            copy.wait_send()
-        product_b(pairs[order], place)
+        if blocking is not None:
+            for copy in blocking:
+                copy.wait_send()
+            product_b(pairs[order], place)
         pl.semaphore_wait(free_x.at[order], EXPERTS - 1)
         xc_copies[order] = []
         for number, (begin, width) in enumerate(parts):
@@ -427,12 +428,16 @@
     loads[1].wait()
     take(0)
     for hop in range(1, 5):
+        if hop == 4:
+            loads[2].wait()
+            for copy in xb_copies[1]:
+                copy.wait_send()
+            product_b(pairs[1], 1)
         gather_step(ring_a, hop, range(4))
         if hop < 4:
             gather_step(ring_g, hop + 1, (0,))
         take(hop)
         if hop == 4:
-            loads[2].wait()
             for copy in sent_a:
                 copy.wait_send()
             for way in range(2):
@@ -440,7 +445,7 @@
         for copy in xb_copies[hop - 1]:
             copy.wait_recv()
         if hop == 4:
-            return_pair(1, 1, xb_copies[1])
+            return_pair(1, 1, None)
         finish(hop - 1)
         if hop == 1:
             give_pair(3)

time: 317 us -> 313 us (0.987)
  Pallas kernels: 315 us -> 310 us
    pallas_call x1, Pallas kernels: 315 us -> 310 us  [per_device(): pl.pallas_call(layer_kernel, out_shape=jax.ShapeDtypeStruct((ROWS, WIDTH)...]
where the time goes in v5:
time: 313 us; the launch traced here: 312 us
  Pallas kernels  310 us (99%)
    pallas_call x1, Pallas kernels, per_device(): pl.pallas_call(layer_kernel, out_shape=jax.ShapeDtypeStruct((ROWS, WIDTH)...  310 us

profile of v5, /device:TPU:1, one launch (start us, length us, event | category | flops | bytes accessed | tf_op | source)
XLA Modules:
  0.0 312.4 jit_solution(3410013763797320783)
XLA Ops:
  0.0 310.2 %layer.1 = bf16[64,7168]{1,0:T(8,128)(2,1)} custom-call(bf16[64,7168]{1,0:T(8,128)(2,1)} %bitcast.15, bf16[1,7168]{1,0:T(2,128)(2,1)} %gain_ref.1, bf16[8,7168]{1,0:T(8,128)(2,1)} %bitcast.16, s32[2,64]{1,0:T(2,128)} %bitcast.17, bf16[7168,256]{1,0:T(8,128)(2,1)} %bitcast.11, bf16[7168,256]{1,0:T(8,128)(2,1)} %bitcast.12, bf16[256,7168]{1,0:T(8,128)(2,1)} %bitcast.13), custom_call_target="tpu_custom_call" | custom-call | tf_op jit(solution)/shard_map/layer/pallas_call | solution.py:623
  310.2 2.2 copy.9

commit v6 on v5

--- a/solution.py
+++ b/solution.py
@@ -133,8 +133,6 @@
         pltpu.make_async_copy(hbm, here, w_sem.at[i])
         for i, (hbm, here) in enumerate(((wg_hbm, wg), (wu_hbm, wu), (wd_hbm, wd)))
     ]
-    for load in loads:
-        load.start()
 
     def start(copy, into):
         copy.start()
@@ -150,16 +148,18 @@
         shifts.append(
             remote(hid_ref.at[:, view], inc.at[:, view], y_send.at[number], y_recv.at[number], after)
         )
+    pl.semaphore_wait(barrier, 1 + 2 + EXPERTS - 1)
+    shifts[0].start()
     squares = jnp.zeros((ROWS, 1), F32)
     for begin, size in chunks:
         values = hid_ref[:, pl.ds(begin, size)].astype(F32)
         squares = squares + jnp.sum(values * values, axis=-1, keepdims=True)
     scale_out[...] = jnp.broadcast_to(lax.rsqrt(squares / WIDTH + 1e-06), (ROWS, LANES))
     scale_copy = remote(scale_out, scale_in, y_send.at[4], y_recv.at[4], after)
-    pl.semaphore_wait(barrier, 1 + 2 + EXPERTS - 1)
     scale_copy.start()
-    shifts[0].start()
     shifts[1].start()
+    for load in loads:
+        load.start()
 
     square = (ROWS, ROWS)
     down, across = lax.broadcasted_iota(jnp.int32, square, 0), lax.broadcasted_iota(jnp.int32, square, 1)

time: 313 us -> 313 us (level)
  no operation moved by 1% of the time
where the time goes in v6:
time: 313 us; the launch traced here: 312 us
  Pallas kernels  310 us (99%)
    pallas_call x1, Pallas kernels, per_device(): pl.pallas_call(layer_kernel, out_shape=jax.ShapeDtypeStruct((ROWS, WIDTH)...  310 us

profile of v6, /device:TPU:1, one launch (start us, length us, event | category | flops | bytes accessed | tf_op | source)
XLA Modules:
  0.0 312.4 jit_solution(7210690672948826736)
XLA Ops:
  0.0 310.2 %layer.1 = bf16[64,7168]{1,0:T(8,128)(2,1)} custom-call(bf16[64,7168]{1,0:T(8,128)(2,1)} %bitcast.15, bf16[1,7168]{1,0:T(2,128)(2,1)} %gain_ref.1, bf16[8,7168]{1,0:T(8,128)(2,1)} %bitcast.16, s32[2,64]{1,0:T(2,128)} %bitcast.17, bf16[7168,256]{1,0:T(8,128)(2,1)} %bitcast.11, bf16[7168,256]{1,0:T(8,128)(2,1)} %bitcast.12, bf16[256,7168]{1,0:T(8,128)(2,1)} %bitcast.13), custom_call_target="tpu_custom_call" | custom-call | tf_op jit(solution)/shard_map/layer/pallas_call | solution.py:623
  310.2 2.2 copy.9
